TPU v7x, 32 devices: a whole 2x2x4 slice. The times are simulated.
32 devices in a mesh: grp: 4 (over y, core), blk: 8 (over z, x).
Axes of the slice: x: 2, y: 2, z: 4, core: 2. Of those that a mesh axis runs over, the one named last changes fastest.
Arguments:
- main_hidden: bfloat16 [1024, 3072], P('blk', 'grp'), may hold values from -6 to 6
- ctrl_query: bfloat16 [1024, 1536], P('blk', 'grp'), may hold values from -150 to 150
- ctrl_key: bfloat16 [1024, 1536], P('blk', 'grp'), may hold values from -6 to 6
- ctrl_value: bfloat16 [1024, 1536], P('blk', 'grp'), may hold values from -6 to 6
- w_out: bfloat16 [1536, 3072], P('grp'), may hold values from -1 to 1
- d_mixed: bfloat16 [1024, 3072], P('blk', 'grp'), may hold values from -3 to 3
- control_slot: int32 [1024], P('blk'), may hold values from 0 to 1023, as said below
Outputs:
- main_mixed: bfloat16 [1024, 3072], P('blk', 'grp')
- d_query: bfloat16 [1024, 1536], P('blk', 'grp')
- d_key: bfloat16 [1024, 1536], P('blk', 'grp')
- d_value: bfloat16 [1024, 1536], P('blk', 'grp')
- d_w_out: float32 [1536, 3072], P('grp', 'blk')
Inputs may be any that keep to these rules, and one draw needn't show every extreme that they name: `control_slot`: A permutation of the token positions. Every aligned block of 128 entries sends exactly 16 of its tokens into each aligned block of 128 control positions.
All inputs are finite; a program needn't handle non-finite values.
Results may differ from a plain program's by a relative error of at most 0.038.
Values may be sent and summed in bfloat16 or wider, within the bound.
A program may use at most 128 MiB of HBM per device.

v0:
```python
import math

import jax
import jax.numpy as jnp
from jax import lax
from jax.sharding import PartitionSpec as P

HD = 128
HEAD_GRP = 3


def on_device(main_hidden, ctrl_query, ctrl_key, ctrl_value, w_out, d_mixed, control_slot):
    rows_dev = ctrl_query.shape[0]
    feature_cols = d_mixed.shape[1]
    blocks = lax.axis_size("blk")
    per_peer = rows_dev // blocks
    score_scale = 1.0 / math.sqrt(HD)
    whole_key, whole_value = (
        lax.all_gather(ctrl_key, "blk", axis=0, tiled=True),
        lax.all_gather(ctrl_value, "blk", axis=0, tiled=True),
    )
    outputs = []
    norm_list = []
    for head_idx in range(HEAD_GRP):
        columns = slice(head_idx * HD, (head_idx + 1) * HD)
        scores = (
            jnp.dot(
                ctrl_query[:, columns], whole_key[:, columns].T, preferred_element_type=jnp.float32
            )
            * score_scale
        )
        row_peak = jnp.max(scores, axis=1, keepdims=True)
        log_norm = row_peak + jnp.log(jnp.sum(jnp.exp(scores - row_peak), axis=1, keepdims=True))
        soft_weights = jnp.exp(scores - log_norm).astype(jnp.bfloat16)
        outputs.append(
            jnp.dot(soft_weights, whole_value[:, columns], preferred_element_type=jnp.float32)
        )
        norm_list.append(log_norm[:, 0])
    attended = jnp.concatenate(outputs, axis=1).astype(jnp.bfloat16)
    log_norms = jnp.stack(norm_list, axis=1)
    target = control_slot // rows_dev
    within = control_slot % rows_dev
    sort_order = jnp.argsort(target)
    inverse = jnp.argsort(sort_order)
    send_within = within[sort_order].reshape(blocks, per_peer)
    arrived, arrived_grad = (
        lax.all_to_all(send_within, "blk", split_axis=0, concat_axis=0, tiled=True),
        lax.all_to_all(
            d_mixed[sort_order].reshape(blocks, per_peer, feature_cols),
            "blk",
            split_axis=0,
            concat_axis=0,
            tiled=True,
        ),
    )
    placed = arrived.reshape(rows_dev)
    grad_rows = jnp.zeros_like(d_mixed).at[placed].set(arrived_grad.reshape(rows_dev, feature_cols))
    residual = lax.psum_scatter(
        jnp.dot(attended, w_out, preferred_element_type=jnp.float32).astype(jnp.bfloat16),
        "grp",
        scatter_dimension=1,
        tiled=True,
    ).astype(jnp.float32)
    returned = lax.all_to_all(
        residual[placed].reshape(blocks, per_peer, feature_cols),
        "blk",
        split_axis=0,
        concat_axis=0,
        tiled=True,
    )
    residual = returned.reshape(rows_dev, feature_cols)[inverse]
    main_mixed = (main_hidden.astype(jnp.float32) + residual).astype(jnp.bfloat16)
    grad_full = lax.all_gather(grad_rows, "grp", axis=1, tiled=True)
    d_proj = jnp.dot(grad_full, w_out.T, preferred_element_type=jnp.float32).astype(jnp.bfloat16)
    d_w_out = lax.psum_scatter(
        jnp.dot(attended.T, grad_full, preferred_element_type=jnp.float32),
        "blk",
        scatter_dimension=1,
        tiled=True,
    )
    row_delta = jnp.sum(
        (d_proj.astype(jnp.float32) * attended.astype(jnp.float32)).reshape(rows_dev, HEAD_GRP, HD),
        axis=2,
    )
    all_norms, all_delta = (
        lax.all_gather(log_norms, "blk", axis=0, tiled=True),
        lax.all_gather(row_delta, "blk", axis=0, tiled=True),
    )
    query_grads = []
    for head_idx in range(HEAD_GRP):
        columns = slice(head_idx * HD, (head_idx + 1) * HD)
        scores = (
            jnp.dot(
                ctrl_query[:, columns], whole_key[:, columns].T, preferred_element_type=jnp.float32
            )
            * score_scale
        )
        soft_weights = jnp.exp(scores - log_norms[:, head_idx : head_idx + 1])
        d_probs = jnp.dot(
            d_proj[:, columns], whole_value[:, columns].T, preferred_element_type=jnp.float32
        )
        d_scores = (soft_weights * (d_probs - row_delta[:, head_idx : head_idx + 1])).astype(
            jnp.bfloat16
        )
        query_grads.append(
            jnp.dot(d_scores, whole_key[:, columns], preferred_element_type=jnp.float32)
            * score_scale
        )
    d_query = jnp.concatenate(query_grads, axis=1).astype(jnp.bfloat16)
    query_piece = lax.all_gather(ctrl_query, "blk", axis=0, tiled=True)
    grad_piece = lax.all_gather(d_proj, "blk", axis=0, tiled=True)
    key_terms = []
    value_terms = []
    for head_idx in range(HEAD_GRP):
        columns = slice(head_idx * HD, (head_idx + 1) * HD)
        scores = (
            jnp.dot(
                query_piece[:, columns], ctrl_key[:, columns].T, preferred_element_type=jnp.float32
            )
            * score_scale
        )
        soft_weights = jnp.exp(scores - all_norms[:, head_idx : head_idx + 1])
        d_probs = jnp.dot(
            grad_piece[:, columns], ctrl_value[:, columns].T, preferred_element_type=jnp.float32
        )
        d_scores = (soft_weights * (d_probs - all_delta[:, head_idx : head_idx + 1])).astype(
            jnp.bfloat16
        )
        key_terms.append(
            jnp.dot(d_scores.T, query_piece[:, columns], preferred_element_type=jnp.float32)
            * score_scale
        )
        value_terms.append(
            jnp.dot(
                soft_weights.astype(jnp.bfloat16).T,
                grad_piece[:, columns],
                preferred_element_type=jnp.float32,
            )
        )
    key_grad = jnp.concatenate(key_terms, axis=1)
    value_grad = jnp.concatenate(value_terms, axis=1)
    return (
        main_mixed,
        d_query,
        key_grad.astype(jnp.bfloat16),
        value_grad.astype(jnp.bfloat16),
        d_w_out,
    )


def solution(mesh):
    in_specs = (
        P("blk", "grp"),
        P("blk", "grp"),
        P("blk", "grp"),
        P("blk", "grp"),
        P("grp", None),
        P("blk", "grp"),
        P("blk"),
    )
    out_specs = (
        P("blk", "grp"),
        P("blk", "grp"),
        P("blk", "grp"),
        P("blk", "grp"),
        P("grp", "blk"),
    )
    return jax.shard_map(
        on_device, mesh=mesh, in_specs=in_specs, out_specs=out_specs, check_vma=False
    )
```

profile of v0, /device:TPU:0, one launch (start us, length us, event | category | flops | bytes accessed | tf_op | source)
XLA Modules:
  0.0 284.0 jit_solution(1283427062478443782)
XLA Ops:
  7.2 34.2 %all_gather.21 = bf16[1024,384]{1,0:T(8,128)(2,1)S(1)} all-gather(bf16[128,384]{1,0:T(8,128)(2,1)} %param.9), channel_id=1, replica_groups=mesh['grp'=4,'blk'=8] {'blk'}, dimensions={0}, use_global_device_ids=true | all-gather | bytes 884736 | tf_op jit(solution)/shard_map/all_gather | solution.py:19
  44.2 32.1 %all_gather.22 = bf16[1024,384]{1,0:T(8,128)(2,1)S(1)} all-gather(bf16[128,384]{1,0:T(8,128)(2,1)S(1)} %copy-done.12), channel_id=1, replica_groups=mesh['grp'=4,'blk'=8] {'blk'}, dimensions={0}, use_global_device_ids=true | all-gather | bytes 884736 | tf_op jit(solution)/shard_map/all_gather | solution.py:20
  79.4 2.5 sort.31
  83.9 5.5 %all-to-all-start = ((s32[8,1,16]{2,1,0:T(1,128)}), s32[8,1,16]{2,1,0:T(1,128)S(1)}, u32[]{:S(2)}, u32[]{:S(2)}) async-start(s32[8,1,16]{2,1,0:T(1,128)} %bitcast), calls=%async_computation.1 | async-start | bytes 8192 | tf_op jit(solution)/shard_map/all_to_all | solution.py:47
  91.0 4.8 %all-to-all-done = s32[8,1,16]{2,1,0:T(1,128)S(1)} async-done(((s32[8,1,16]{2,1,0:T(1,128)}), s32[8,1,16]{2,1,0:T(1,128)S(1)}, u32[]{:S(2)}, u32[]{:S(2)}) %all-to-all-start) | async-done | bytes 544 | tf_op jit(solution)/shard_map/all_to_all | solution.py:47
  95.8 3.4 %all-to-all-start.2 = ((bf16[8,16,768]{2,1,0:T(8,128)(2,1)}), bf16[8,16,768]{2,1,0:T(8,128)(2,1)S(1)}, u32[]{:S(2)}, u32[]{:S(2)}) async-start(bf16[8,16,768]{2,1,0:T(8,128)(2,1)} %bitcast.4), calls=%async_computation.3 | async-start | bytes 393216 | tf_op jit(solution)/shard_map/all_to_all | solution.py:48
  100.5 6.4 %all-to-all-done.2 = bf16[8,16,768]{2,1,0:T(8,128)(2,1)S(1)} async-done(((bf16[8,16,768]{2,1,0:T(8,128)(2,1)}), bf16[8,16,768]{2,1,0:T(8,128)(2,1)S(1)}, u32[]{:S(2)}, u32[]{:S(2)}) %all-to-all-start.2) | async-done | bytes 196640 | tf_op jit(solution)/shard_map/all_to_all | solution.py:48
  108.1 8.6 %all_gather.23 = bf16[128,3072]{1,0:T(8,128)(2,1)S(1)} all-gather(bf16[128,768]{1,0:T(8,128)(2,1)S(1)} %scatter_custom_fusion), channel_id=1, replica_groups=mesh['grp'=4,'blk'=8] {'grp'}, dimensions={1}, use_global_device_ids=true | all-gather | bytes 983040 | tf_op jit(solution)/shard_map/all_gather | solution.py:73
  117.6 2.9 %fusion.108 = f32[384,3072]{1,0:T(8,128)} fusion(bf16[128,3072]{1,0:T(8,128)(2,1)S(1)} %all_gather.23, bf16[128,128]{0,1:T(8,128)(2,1)S(1)} %convolution_convert_fusion.5, bf16[128,128]{0,1:T(8,128)(2,1)S(1)} %convolution_convert_fusion.6, bf16[128,128]{0,1:T(8,128)(2,1)S(1)} %convolution_convert_fusion.7), kind=kOutput, calls=%fused_computation.148 | convolution fusion | flops 302284800 | bytes 5603328 | tf_op jit(solution)/shard_map/dot_general | solution.py:76
  120.5 2.5 sort.32
  123.1 26.9 %all_gather.25 = f32[1024,3]{0,1:T(4,128)S(1)} all-gather(f32[128,3]{0,1:T(4,128)S(1)} %pad_maximum_fusion.4), channel_id=1, replica_groups=mesh['grp'=4,'blk'=8] {'blk'}, dimensions={0}, use_global_device_ids=true | all-gather | bytes 13824 | tf_op jit(solution)/shard_map/all_gather | solution.py:86
  150.0 33.9 %all_gather.24 = bf16[1024,384]{1,0:T(8,128)(2,1)S(1)} all-gather(bf16[128,384]{1,0:T(8,128)(2,1)S(1)} %copy-done.10), channel_id=1, replica_groups=mesh['grp'=4,'blk'=8] {'blk'}, dimensions={0}, use_global_device_ids=true | all-gather | bytes 884736 | tf_op jit(solution)/shard_map/all_gather | solution.py:110
  187.2 1.9 convert_multiply_fusion
  189.2 1.6 fusion.32
  190.8 1.7 fusion.31
  192.6 1.7 fusion.30
  195.0 27.4 %all_gather.27 = f32[1024,3]{0,1:T(4,128)S(1)} all-gather(f32[128,3]{0,1:T(4,128)S(1)} %reduce_sum.39), channel_id=1, replica_groups=mesh['grp'=4,'blk'=8] {'blk'}, dimensions={0}, use_global_device_ids=true | all-gather | bytes 13824 | tf_op jit(solution)/shard_map/all_gather | solution.py:87
  222.4 28.5 %all_gather.26 = bf16[1024,384]{0,1:T(8,128)(2,1)S(1)} all-gather(bf16[128,384]{0,1:T(8,128)(2,1)S(1)} %get-tuple-element.42), channel_id=1, replica_groups=mesh['grp'=4,'blk'=8] {'blk'}, dimensions={0}, use_global_device_ids=true | all-gather | bytes 884736 | tf_op jit(solution)/shard_map/all_gather | solution.py:111
  251.8 1.9 convolution_convert_fusion.2
  253.7 2.3 fusion.35
  256.0 2.3 fusion.34
  258.3 2.3 fusion.33
  263.1 3.5 %all-to-all-start.1 = ((f32[8,16,768]{2,1,0:T(8,128)}), f32[8,16,768]{2,1,0:T(8,128)S(1)}, u32[]{:S(2)}, u32[]{:S(2)}) async-start(f32[8,16,768]{2,1,0:T(8,128)} %bitcast.28), calls=%async_computation.2 | async-start | bytes 786432 | tf_op jit(solution)/shard_map/all_to_all | solution.py:64
  273.7 2.0 all-to-all-done.1
  (91 shorter events, 28.8 us)
Async XLA Ops:
  7.2 70.7 %copy-start = (bf16[384,3072]{1,0:T(8,128)(2,1)S(1)}, bf16[384,3072]{1,0:T(8,128)(2,1)}, u32[]{:S(2)}) copy-start(bf16[384,3072]{1,0:T(8,128)(2,1)} %param.11) | copy-start | bytes 7077892
  7.2 36.4 %copy-start.10 = (bf16[128,384]{1,0:T(8,128)(2,1)S(1)}, bf16[128,384]{1,0:T(8,128)(2,1)}, u32[]{:S(2)}) copy-start(bf16[128,384]{1,0:T(8,128)(2,1)} %param.8) | copy-start | bytes 294916
  7.2 37.0 %copy-start.12 = (bf16[128,384]{1,0:T(8,128)(2,1)S(1)}, bf16[128,384]{1,0:T(8,128)(2,1)}, u32[]{:S(2)}) copy-start(bf16[128,384]{1,0:T(8,128)(2,1)} %param.10) | copy-start | bytes 294916
  7.2 253.3 %reduce-scatter.3.cloned.1.call-start = ((), (), s32[]{:S(2)}) async-start(), calls=%async_computation.5 | async-start | bytes 983040 | tf_op jit(solution)/shard_map/reduce_scatter | solution.py:58
  41.4 2.2 copy-start.8
  42.5 34.7 %copy-start.7 = (f32[128,1024]{1,0:T(8,128)}, f32[128,1024]{1,0:T(8,128)S(1)}, u32[]{:S(2)}) copy-start(f32[128,1024]{1,0:T(8,128)S(1)} %get-tuple-element.36) | copy-start | bytes 1572868
  43.6 33.9 %copy-start.6 = (f32[128,1024]{1,0:T(8,128)}, f32[128,1024]{1,0:T(8,128)S(1)}, u32[]{:S(2)}) copy-start(f32[128,1024]{1,0:T(8,128)S(1)} %get-tuple-element.38) | copy-start | bytes 1572868
  43.9 33.6 %copy-start.5 = (f32[128,1024]{1,0:T(8,128)}, f32[128,1024]{1,0:T(8,128)S(1)}, u32[]{:S(2)}) copy-start(f32[128,1024]{1,0:T(8,128)S(1)} %get-tuple-element.40) | copy-start | bytes 1572868
  76.3 1.2 copy-start.9
  76.5 46.5 %copy-start.15 = (f32[128]{0:T(128)}, f32[128]{0:T(128)S(1)}, u32[]{:S(2)}) copy-start(f32[128]{0:T(128)S(1)} %log_add_fusion.1) | copy-start | bytes 1540
  77.5 45.6 %copy-start.16 = (f32[128]{0:T(128)}, f32[128]{0:T(128)S(1)}, u32[]{:S(2)}) copy-start(f32[128]{0:T(128)S(1)} %log_add_fusion.2) | copy-start | bytes 1540
  77.5 1.9 copy-start.17
  77.9 11.6 %copy-start.1 = (bf16[128,768]{1,0:T(8,128)(2,1)S(1)}, bf16[128,768]{1,0:T(8,128)(2,1)}, u32[]{:S(2)}) copy-start(bf16[128,768]{1,0:T(8,128)(2,1)} %param.12) | copy-start | bytes 589828
  83.9 11.9 %all-to-all-start = ((s32[8,1,16]{2,1,0:T(1,128)}), s32[8,1,16]{2,1,0:T(1,128)S(1)}, u32[]{:S(2)}, u32[]{:S(2)}) async-start(s32[8,1,16]{2,1,0:T(1,128)} %bitcast), calls=%async_computation.1 | async-start | bytes 8192 | tf_op jit(solution)/shard_map/all_to_all | solution.py:47
  95.8 11.1 %all-to-all-start.2 = ((bf16[8,16,768]{2,1,0:T(8,128)(2,1)}), bf16[8,16,768]{2,1,0:T(8,128)(2,1)S(1)}, u32[]{:S(2)}, u32[]{:S(2)}) async-start(bf16[8,16,768]{2,1,0:T(8,128)(2,1)} %bitcast.4), calls=%async_computation.3 | async-start | bytes 393216 | tf_op jit(solution)/shard_map/all_to_all | solution.py:48
  99.2 178.0 %reduce-scatter.5.cloned.1.call-start = ((), (), s32[]{:S(2)}) async-start(), calls=%async_computation.6 | async-start | bytes 5308416 | tf_op jit(solution)/shard_map/reduce_scatter | solution.py:75
  116.7 0.9 copy-start.4
  120.5 63.5 %copy-start.11 = (bf16[128,384]{1,0:T(8,128)(2,1)S(1)}, bf16[128,384]{1,0:T(8,128)(2,1)}, u32[]{:S(2)}) copy-start(bf16[128,384]{1,0:T(8,128)(2,1)} %param.9) | copy-start | bytes 294916
  190.8 62.9 %copy-start.13 = (bf16[128,384]{1,0:T(8,128)(2,1)S(1)}, bf16[128,384]{1,0:T(8,128)(2,1)}, u32[]{:S(2)}) copy-start(bf16[128,384]{1,0:T(8,128)(2,1)} %param.10) | copy-start | bytes 294916
  250.9 0.9 copy-start.2
  261.5 8.1 %copy-start.3 = (bf16[1024,384]{0,1:T(8,128)(2,1)S(1)}, bf16[1024,384]{0,1:T(8,128)(2,1)}, u32[]{:S(2)}) copy-start(bf16[1024,384]{0,1:T(8,128)(2,1)} %copy-done.2) | copy-start | bytes 2359300
  263.1 12.6 %all-to-all-start.1 = ((f32[8,16,768]{2,1,0:T(8,128)}), f32[8,16,768]{2,1,0:T(8,128)S(1)}, u32[]{:S(2)}, u32[]{:S(2)}) async-start(f32[8,16,768]{2,1,0:T(8,128)} %bitcast.28), calls=%async_computation.2 | async-start | bytes 786432 | tf_op jit(solution)/shard_map/all_to_all | solution.py:64
  272.1 4.4 %copy-start.14 = (bf16[128,768]{1,0:T(8,128)(2,1)S(1)}, bf16[128,768]{1,0:T(8,128)(2,1)}, u32[]{:S(2)}) copy-start(bf16[128,768]{1,0:T(8,128)(2,1)} %param.7) | copy-start | bytes 589828
Sparse Core Ops, SparseCore 0:
  79.5 24.2 reduce-scatter.2
  120.6 101.3 reduce-scatter.4
where the time goes:
time: 285 us; the launch traced here: 284 us
  blocking collectives  192 us (67%)
  matrix products  29.2 us (10%)
  between operations  14.4 us (5%)
  waiting for transfers between devices  13.2 us (5%)
  local copies, waits for them, and re-layouts  12.7 us (4%)
  starting transfers between devices  12.5 us (4%)
  other arithmetic  10.4 us (4%)
    all_gather x1, blocking collectives, on_device(): lax.all_gather(ctrl_key, 'blk', axis=0, tiled=True)  34.2 us
    all_gather x1, blocking collectives, on_device(): query_piece = lax.all_gather(ctrl_query, 'blk', axis=0, tiled=True)  33.9 us
    all_gather x1, blocking collectives, on_device(): lax.all_gather(ctrl_value, 'blk', axis=0, tiled=True)  32.1 us
    all_gather x1, blocking collectives, on_device(): grad_piece = lax.all_gather(d_proj, 'blk', axis=0, tiled=True)  28.5 us
    all_gather x1, blocking collectives, on_device(): lax.all_gather(row_delta, 'blk', axis=0, tiled=True)  27.4 us
    all_gather x1, blocking collectives, on_device(): lax.all_gather(log_norms, 'blk', axis=0, tiled=True)  26.9 us
    all_gather x1, blocking collectives, on_device(): grad_full = lax.all_gather(grad_rows, 'grp', axis=1, tiled=True)  8.63 us
    dot_general x3, matrix products, on_device(): jnp.dot(d_scores.T, query_piece[:, columns], preferred_element_type=jnp.f...  6.8 us
  transfers between devices with their start and end apart: 5, of which 3 were waited for; matrix products, arithmetic and copies ran while one was open for 16% of the time, Pallas kernels for 0%

commit v1 on v0

--- a/solution.py
+++ b/solution.py
@@ -148,6 +148,73 @@
     )
 
 
+def on_device_small(main_hidden, ctrl_query, ctrl_key, ctrl_value, w_out, d_mixed, control_slot):
+    f32, bf16 = jnp.float32, jnp.bfloat16
+    rows_dev = ctrl_query.shape[0]
+    blocks = lax.axis_size("blk")
+    seq = rows_dev * blocks
+    width = ctrl_query.shape[1]
+    cols = w_out.shape[1] // blocks
+    score_scale = 1.0 / math.sqrt(HD)
+    me = lax.axis_index("blk")
+
+    qkv = lax.all_gather(
+        jnp.concatenate([ctrl_query, ctrl_key, ctrl_value], axis=1), "blk", axis=0, tiled=True
+    )
+    grad_full = lax.all_gather(d_mixed, "grp", axis=1, tiled=True)
+    slots = lax.all_gather(control_slot, "blk", axis=0, tiled=True)
+    to_main = (slots[:, None] == lax.broadcasted_iota(jnp.int32, (seq, seq), 1)).astype(bf16)
+    d_proj_main = jnp.dot(grad_full, w_out.T, preferred_element_type=f32).astype(bf16)
+    grad_cols = lax.all_to_all(
+        grad_full.reshape(rows_dev, blocks, cols), "blk", split_axis=1, concat_axis=0, tiled=True
+    ).reshape(seq, cols)
+    d_proj_main = lax.all_gather(d_proj_main, "blk", axis=0, tiled=True)
+    d_proj_all = jnp.dot(to_main.T, d_proj_main, preferred_element_type=f32).astype(bf16)
+
+    whole_query, whole_key, whole_value = (qkv[:, i * width : (i + 1) * width] for i in range(3))
+    outs, norms, weights = [], [], []
+    for h in range(HEAD_GRP):
+        c = slice(h * HD, (h + 1) * HD)
+        scores = jnp.dot(ctrl_query[:, c], whole_key[:, c].T, preferred_element_type=f32) * score_scale
+        peak = jnp.max(scores, axis=1, keepdims=True)
+        log_norm = peak + jnp.log(jnp.sum(jnp.exp(scores - peak), axis=1, keepdims=True))
+        p = jnp.exp(scores - log_norm)
+        outs.append(jnp.dot(p.astype(bf16), whole_value[:, c], preferred_element_type=f32))
+        norms.append(log_norm)
+        weights.append(p)
+    attended = jnp.concatenate(outs, axis=1).astype(bf16)
+    norms = jnp.concatenate(norms, axis=1)
+    attended_all = lax.all_gather(attended, "blk", axis=0, tiled=True)
+    norms_all = lax.all_gather(norms, "blk", axis=0, tiled=True)
+
+    attended_main = jnp.dot(to_main, attended_all, preferred_element_type=f32).astype(bf16)
+    own_main = lax.dynamic_slice_in_dim(attended_main, me * rows_dev, rows_dev, 0)
+    partial = jnp.dot(own_main, w_out, preferred_element_type=f32).astype(bf16)
+    residual = lax.psum_scatter(partial, "grp", scatter_dimension=1, tiled=True)
+    main_mixed = (main_hidden.astype(f32) + residual.astype(f32)).astype(bf16)
+    d_w_out = jnp.dot(attended_main.T, grad_cols, preferred_element_type=f32)
+
+    delta_all = jnp.sum(
+        (d_proj_all.astype(f32) * attended_all.astype(f32)).reshape(seq, HEAD_GRP, HD), axis=2
+    )
+    d_proj = lax.dynamic_slice_in_dim(d_proj_all, me * rows_dev, rows_dev, 0)
+    delta = lax.dynamic_slice_in_dim(delta_all, me * rows_dev, rows_dev, 0)
+    dq, dk, dv = [], [], []
+    for h in range(HEAD_GRP):
+        c = slice(h * HD, (h + 1) * HD)
+        d_probs = jnp.dot(d_proj[:, c], whole_value[:, c].T, preferred_element_type=f32)
+        d_scores = (weights[h] * (d_probs - delta[:, h : h + 1])).astype(bf16)
+        dq.append(jnp.dot(d_scores, whole_key[:, c], preferred_element_type=f32) * score_scale)
+        scores = jnp.dot(whole_query[:, c], ctrl_key[:, c].T, preferred_element_type=f32) * score_scale
+        p = jnp.exp(scores - norms_all[:, h : h + 1])
+        d_probs = jnp.dot(d_proj_all[:, c], ctrl_value[:, c].T, preferred_element_type=f32)
+        d_scores = (p * (d_probs - delta_all[:, h : h + 1])).astype(bf16)
+        dk.append(jnp.dot(d_scores.T, whole_query[:, c], preferred_element_type=f32) * score_scale)
+        dv.append(jnp.dot(p.astype(bf16).T, d_proj_all[:, c], preferred_element_type=f32))
+    dq, dk, dv = (jnp.concatenate(x, axis=1).astype(bf16) for x in (dq, dk, dv))
+    return main_mixed, dq, dk, dv, d_w_out
+
+
 def solution(mesh):
     in_specs = (
         P("blk", "grp"),
@@ -165,6 +232,7 @@
         P("blk", "grp"),
         P("grp", "blk"),
     )
+    body = on_device_small if mesh.shape["blk"] <= 8 else on_device
     return jax.shard_map(
-        on_device, mesh=mesh, in_specs=in_specs, out_specs=out_specs, check_vma=False
-    )
+        body, mesh=mesh, in_specs=in_specs, out_specs=out_specs, check_vma=False
+    )

time: 285 us -> 211 us (0.74)
  blocking collectives: 192 us -> 134 us
  waiting for transfers between devices: 13.2 us -> 0.04 us
  matrix products: 29.2 us -> 42.3 us
  local copies, waits for them, and re-layouts: 12.7 us -> 6.01 us
  starting transfers between devices: 12.5 us -> 5.88 us
    all_gather x7 -> x5, blocking collectives: 192 us -> 134 us  [the longest x1 35.2 us: on_device_small(): d_proj_main = lax.all_gather(d_proj_main, 'blk', axis=0, tiled=True)]
    all_to_all x3 -> x1, waiting for transfers between devices: 13.2 us -> 0.01 us  [on_device_small(): lax.all_to_all(grad_full.reshape(rows_dev, blocks, cols), 'blk', split_ax...]
    dot_general x21 -> x23, matrix products: 29.2 us -> 42.3 us  [the longest x3 6.47 us: on_device_small(): jnp.dot(d_scores, whole_key[:, c], preferred_element_type=f32) * score_scale]
    all_to_all x3 -> x1, starting transfers between devices: 12.4 us -> 5.81 us  [on_device_small(): lax.all_to_all(grad_full.reshape(rows_dev, blocks, cols), 'blk', split_ax...]
    gather x4 -> x0, local copies, waits for them, and re-layouts: 5.16 us -> none  [the longest x1 1.57 us: on_device(): residual[placed].reshape(blocks, per_peer, feature_cols)]
    sort x2 -> x0, other arithmetic: 5.07 us -> none  [the longest x1 2.54 us: on_device(): sort_order = jnp.argsort(target)]
  transfers between devices with their start and end apart: 5 -> 3, of which waited for: 3 -> 0; matrix products, arithmetic and copies ran while one was open for 16% -> 17% of each run, Pallas kernels for 0% -> 0%
where the time goes in v1:
time: 211 us; the launch traced here: 210 us
  blocking collectives  134 us (64%)
  matrix products  42.3 us (20%)
  between operations  14.2 us (7%)
  other arithmetic  7.8 us (4%)
  local copies, waits for them, and re-layouts  6.01 us (3%)
  starting transfers between devices  5.88 us (3%)
    all_gather x1, blocking collectives, on_device_small(): d_proj_main = lax.all_gather(d_proj_main, 'blk', axis=0, tiled=True)  35.2 us
    all_gather x1, blocking collectives, on_device_small(): slots = lax.all_gather(control_slot, 'blk', axis=0, tiled=True)  33.2 us
    all_gather x1, blocking collectives, on_device_small(): attended_all = lax.all_gather(attended, 'blk', axis=0, tiled=True)  28.7 us
    all_gather x1, blocking collectives, on_device_small(): norms_all = lax.all_gather(norms, 'blk', axis=0, tiled=True)  26 us
    all_gather x1, blocking collectives, on_device_small(): grad_full = lax.all_gather(d_mixed, 'grp', axis=1, tiled=True)  10.5 us
    dot_general x3, matrix products, on_device_small(): jnp.dot(d_scores, whole_key[:, c], preferred_element_type=f32) * score_scale  6.47 us
    dot_general x3, matrix products, on_device_small(): jnp.dot(d_scores.T, whole_query[:, c], preferred_element_type=f32)  6.47 us
    dot_general x3, matrix products, on_device_small(): jnp.dot(whole_query[:, c], ctrl_key[:, c].T, preferred_element_type=f32)  6.05 us
  transfers between devices with their start and end apart: 3, of which 0 were waited for; matrix products, arithmetic and copies ran while one was open for 17% of the time, Pallas kernels for 0%

profile of v1, /device:TPU:0, one launch (start us, length us, event | category | flops | bytes accessed | tf_op | source)
XLA Modules:
  0.0 209.9 jit_solution(4451264742679285016)
XLA Ops:
  7.2 1.9 pad_maximum_fusion
  10.2 10.5 %all_gather.21 = bf16[128,3072]{0,1:T(8,128)(2,1)} all-gather(bf16[128,768]{0,1:T(8,128)(2,1)S(1)} %copy.26), channel_id=1, replica_groups=mesh['grp'=4,'blk'=8] {'grp'}, dimensions={1}, use_global_device_ids=true | all-gather | bytes 983040 | tf_op jit(solution)/shard_map/all_gather | solution.py:164
  20.8 5.8 %all-to-all-start = ((bf16[128,8,384]{0,2,1:T(8,128)(2,1)}), bf16[128,8,384]{0,2,1:T(8,128)(2,1)S(1)}, u32[]{:S(2)}, u32[]{:S(2)}) async-start(bf16[128,8,384]{0,2,1:T(8,128)(2,1)} %bitcast.18), calls=%async_computation.1 | async-start | bytes 1572864 | tf_op jit(solution)/shard_map/all_to_all | solution.py:168
  26.6 33.2 %all-gather = s32[8,1,128]{2,1,0:T(1,128)S(1)} all-gather(s32[1,1,128]{2,1,0:T(1,128)S(1)} %bitcast.65), channel_id=1, replica_groups=mesh['grp'=4,'blk'=8] {'blk'}, dimensions={0}, use_global_device_ids=true | all-gather | bytes 4608 | tf_op jit(solution)/shard_map/all_gather | solution.py:165
  59.9 2.0 convolution_convert_fusion.1
  61.9 35.2 %all_gather.22 = bf16[1024,384]{1,0:T(8,128)(2,1)} all-gather(bf16[128,384]{1,0:T(8,128)(2,1)S(1)} %convolution_convert_fusion.1), channel_id=1, replica_groups=mesh['grp'=4,'blk'=8] {'blk'}, dimensions={0}, use_global_device_ids=true | all-gather | bytes 884736 | tf_op jit(solution)/shard_map/all_gather | solution.py:171
  106.3 28.7 %all_gather.20 = bf16[1024,384]{0,1:T(8,128)(2,1)S(1)} all-gather(bf16[128,384]{0,1:T(8,128)(2,1)S(1)} %pad_maximum_fusion.1), channel_id=1, replica_groups=mesh['grp'=4,'blk'=8] {'blk'}, dimensions={0}, use_global_device_ids=true | all-gather | bytes 884736 | tf_op jit(solution)/shard_map/all_gather | solution.py:187
  135.0 2.2 %fusion.4 = bf16[1024,384]{1,0:T(8,128)(2,1)} fusion(bf16[1024,384]{0,1:T(8,128)(2,1)S(1)} %all_gather.20, s32[1024]{0:T(1024)S(1)} %bitcast.60), kind=kOutput, calls=%fused_computation.7 | convolution fusion | flops 806748160 | bytes 1576960 | tf_op jit(solution)/shard_map/dot_general | solution.py:190
  137.2 2.7 %convert_multiply_fusion = (f32[1024,384]{0,1:T(8,128)}, bf16[1024,384]{0,1:T(8,128)(2,1)}) fusion(bf16[1024,384]{0,1:T(8,128)(2,1)S(1)} %all_gather.20, bf16[1024,384]{1,0:T(8,128)(2,1)S(1)} %copy-done.4, s32[1024]{0:T(1024)S(1)} %bitcast.61), kind=kOutput, calls=%fused_computation.6 | convolution fusion | flops 807927808 | bytes 3936256 | tf_op jit(solution)/shard_map/dot_general | solution.py:172
  139.9 1.5 reduce_sum.39
  141.5 2.4 %convolution_convert_fusion = bf16[128,3072]{1,0:T(8,128)(2,1)} fusion(bf16[384,3072]{1,0:T(8,128)(2,1)S(1)} %copy-done, bf16[1024,384]{1,0:T(8,128)(2,1)} %fusion.4, s32[]{:T(128)S(6)} %select_n.2), kind=kOutput, calls=%fused_computation.3 | convolution fusion | flops 302383104 | bytes 3244036 | tf_op jit(solution)/shard_map/dot_general | solution.py:192
  144.4 26.0 %all_gather.23 = f32[1024,3]{0,1:T(4,128)S(1)} all-gather(f32[128,3]{0,1:T(4,128)S(1)} %pad_maximum_fusion.5), channel_id=1, replica_groups=mesh['grp'=4,'blk'=8] {'blk'}, dimensions={0}, use_global_device_ids=true | all-gather | bytes 13824 | tf_op jit(solution)/shard_map/all_gather | solution.py:188
  170.5 2.0 fusion.13
  172.5 2.0 fusion.10
  174.5 2.0 fusion.7
  176.5 2.3 %fusion.39 = bf16[128,128]{0,1:T(8,128)(2,1)} fusion(f32[1024,128]{1,0:T(8,128)} %copy-done.1, f32[128]{0:T(128)S(1)} %copy-done.10, f32[128]{0:T(128)S(1)} %log_add_fusion.2, bf16[1024,1152]{1,0:T(8,128)(2,1)} %all-gather.3.cloned.1.call-done, bf16[1024,384]{0,1:T(8,128)(2,1)} %get-tuple-element.41, s32[]{:T(128)S(6)} %select_n.2), kind=kOutput, calls=%fused_computation.55 | convolution fusion | flops 67665920 | bytes 1115140 | tf_op jit(solution)/shard_map/dot_general | solution.py:207
  178.8 2.1 fusion.41
  180.9 2.1 fusion.40
  183.0 1.8 fusion.38
  184.8 2.3 %fusion.37 = bf16[128,128]{0,1:T(8,128)(2,1)} fusion(f32[1024,128]{1,0:T(8,128)} %fusion.10, f32[1024]{0:T(1024)S(1)} %bitcast.55, bf16[1024,384]{0,1:T(8,128)(2,1)} %get-tuple-element.41, bf16[1024,1152]{1,0:T(8,128)(2,1)} %all-gather.3.cloned.1.call-done, bf16[128,384]{1,0:T(8,128)(2,1)S(1)} %copy-done.7), kind=kOutput, calls=%fused_computation.53 | convolution fusion | flops 67534848 | bytes 1118208 | tf_op jit(solution)/shard_map/dot_general | solution.py:212
  188.6 1.6 copy.31
  190.2 2.3 %fusion.36 = bf16[128,128]{0,1:T(8,128)(2,1)} fusion(f32[1024,128]{1,0:T(8,128)} %fusion.7, f32[1024]{0:T(1024)S(1)} %bitcast.54, bf16[1024,384]{0,1:T(8,128)(2,1)} %get-tuple-element.41, bf16[1024,1152]{1,0:T(8,128)(2,1)} %all-gather.3.cloned.1.call-done, bf16[128,384]{1,0:T(8,128)(2,1)S(1)} %copy-done.7), kind=kOutput, calls=%fused_computation.52 | convolution fusion | flops 67534848 | bytes 1118208 | tf_op jit(solution)/shard_map/dot_general | solution.py:212
  198.6 2.8 %fusion.117 = f32[384,384]{1,0:T(8,128)} fusion(bf16[1024,384]{1,0:T(8,128)(2,1)} %fusion.4, bf16[1024,384]{1,0:T(8,128)(2,1)} %bitcast.53), kind=kOutput, calls=%fused_computation.149 | convolution fusion | flops 301989888 | bytes 2162688 | tf_op jit(solution)/shard_map/dot_general | solution.py:195
  201.4 1.7 add_convert_fusion
  (57 shorter events, 18.4 us)
Async XLA Ops:
  7.2 52.7 %copy-start = (bf16[384,3072]{1,0:T(8,128)(2,1)S(1)}, bf16[384,3072]{1,0:T(8,128)(2,1)}, u32[]{:S(2)}) copy-start(bf16[384,3072]{1,0:T(8,128)(2,1)} %param.11) | copy-start | bytes 7077892
  7.2 19.4 %copy-start.9 = (s32[128]{0:T(128)S(1)}, s32[128]{0:T(128)}, u32[]{:S(2)}) copy-start(s32[128]{0:T(128)} %param.13) | copy-start | bytes 1540
  7.2 91.1 %all-gather.3.cloned.1.call-start = ((), (), s32[]{:S(2)}) async-start(), calls=%async_computation.2 | async-start | bytes 2654208 | tf_op jit(solution)/shard_map/all_gather | solution.py:161
  20.8 76.3 %all-to-all-start = ((bf16[128,8,384]{0,2,1:T(8,128)(2,1)}), bf16[128,8,384]{0,2,1:T(8,128)(2,1)S(1)}, u32[]{:S(2)}, u32[]{:S(2)}) async-start(bf16[128,8,384]{0,2,1:T(8,128)(2,1)} %bitcast.18), calls=%async_computation.1 | async-start | bytes 1572864 | tf_op jit(solution)/shard_map/all_to_all | solution.py:168
  26.6 174.8 %reduce-scatter.2.cloned.1.call-start = ((), (), s32[]{:S(2)}) async-start(), calls=%async_computation.3 | async-start | bytes 983040 | tf_op jit(solution)/shard_map/reduce_scatter | solution.py:193
  59.9 38.4 %copy-start.5 = (bf16[128,384]{1,0:T(8,128)(2,1)S(1)}, bf16[128,384]{1,0:T(8,128)(2,1)}, u32[]{:S(2)}) copy-start(bf16[128,384]{1,0:T(8,128)(2,1)} %param.8) | copy-start | bytes 294916
  102.4 2.7 %copy-start.1 = (f32[1024,128]{1,0:T(8,128)}, f32[1024,128]{1,0:T(8,128)S(1)}, u32[]{:S(2)}) copy-start(f32[1024,128]{1,0:T(8,128)S(1)} %get-tuple-element.39) | copy-start | bytes 1572868
  135.0 2.2 %copy-start.4 = (bf16[1024,384]{1,0:T(8,128)(2,1)S(1)}, bf16[1024,384]{1,0:T(8,128)(2,1)}, u32[]{:S(2)}) copy-start(bf16[1024,384]{1,0:T(8,128)(2,1)} %all_gather.22) | copy-start | bytes 2359300
  141.5 29.0 %copy-start.6 = (bf16[128,384]{1,0:T(8,128)(2,1)S(1)}, bf16[128,384]{1,0:T(8,128)(2,1)}, u32[]{:S(2)}) copy-start(bf16[128,384]{1,0:T(8,128)(2,1)} %param.9) | copy-start | bytes 294916
  144.4 32.1 %copy-start.10 = (f32[128]{0:T(128)S(1)}, f32[128]{0:T(128)}, u32[]{:S(2)}) copy-start(f32[128]{0:T(128)} %get-tuple-element.31) | copy-start | bytes 1540
  176.5 6.5 %copy-start.7 = (bf16[128,384]{1,0:T(8,128)(2,1)S(1)}, bf16[128,384]{1,0:T(8,128)(2,1)}, u32[]{:S(2)}) copy-start(bf16[128,384]{1,0:T(8,128)(2,1)} %param.10) | copy-start | bytes 294916
  183.0 11.1 %copy-start.2 = (f32[1024,128]{1,0:T(8,128)S(1)}, f32[1024,128]{1,0:T(8,128)}, u32[]{:S(2)}) copy-start(f32[1024,128]{1,0:T(8,128)} %fusion.13) | copy-start | bytes 1572868
  183.0 12.3 %copy-start.3 = (f32[1024,128]{1,0:T(8,128)S(1)}, f32[1024,128]{1,0:T(8,128)}, u32[]{:S(2)}) copy-start(f32[1024,128]{1,0:T(8,128)} %fusion.10) | copy-start | bytes 1572868
  195.3 6.1 %copy-start.8 = (bf16[128,768]{1,0:T(8,128)(2,1)S(1)}, bf16[128,768]{1,0:T(8,128)(2,1)}, u32[]{:S(2)}) copy-start(bf16[128,768]{1,0:T(8,128)(2,1)} %param.7) | copy-start | bytes 589828
Sparse Core Ops, SparseCore 0:
  10.8 65.2 all-gather.2
  144.0 20.6 reduce-scatter.1

commit v2 on v0

--- a/solution.py
+++ b/solution.py
@@ -1,8 +1,11 @@
+import functools
 import math
 
 import jax
 import jax.numpy as jnp
 from jax import lax
+from jax.experimental import pallas as pl
+from jax.experimental.pallas import tpu as pltpu
 from jax.sharding import PartitionSpec as P
 
 HD = 128
@@ -148,6 +151,371 @@
     )
 
 
+F32, BF16 = jnp.float32, jnp.bfloat16
+
+
+def dot(a, b, ca, cb):
+    return lax.dot_general(a, b, (((ca,), (cb,)), ((), ())), preferred_element_type=F32)
+
+
+def fused_kernel(
+    hidden_ref, q_ref, k_ref, v_ref, w_ref, dm_ref, slot_ref,
+    mixed_ref, dq_ref, dk_ref, dv_ref, dw_ref,
+    dm_full, qkv_in, slots_in, dp_send, do_in, do_ctrl, d_cols,
+    probs, place, att_ctrl, att_send, att_all, rs_send, rs_in,
+    dk_acc, dv_acc, grad_send, grad_in,
+    s_dm, s_qkv, s_slot, s_do, s_ca, s_cb, s_at, s_ag, s_rs, s_gr,
+    r_dm, r_qkv, r_slot, r_do, r_ca, r_cb, r_at, r_ag, r_rs, r_gr,
+):
+    g = lax.axis_index("grp")
+    b = lax.axis_index("blk")
+    n_grp, blocks = dm_full.shape[0], qkv_in.shape[1]
+    rows, feat = dm_ref.shape
+    cols = d_cols.shape[3]
+    quarter = rows // n_grp
+    seq = rows * blocks
+    chunks = 4
+    per = blocks // chunks
+    step = seq // chunks
+    scale = 1.0 / math.sqrt(HD)
+    c = g % 2
+    z, x = b // 2, b % 2
+    nz = blocks // 2
+    mate = b + 1 - 2 * x
+    owners = [2 + 2 * c, 5 - 2 * c, 7 * c]
+    mine = jnp.where(b == owners[1], 1, jnp.where(b == owners[2], 2, 0))
+    is_owner = (b == owners[0]) | (b == owners[1]) | (b == owners[2])
+    pending = []
+
+    def remote(src, dst, ss, rs, dev):
+        return pltpu.make_async_remote_copy(
+            src_ref=src, dst_ref=dst, send_sem=ss, recv_sem=rs,
+            device_id=dev, device_id_type=pl.DeviceIdType.MESH,
+        )
+
+    def send(cond, make):
+        pl.when(cond)(lambda: make().start())
+        pending.append((cond, make))
+
+    def arrive(cond, make):
+        pl.when(cond)(lambda: make().wait_recv())
+
+    barrier = pltpu.get_barrier_semaphore()
+    for d in range(1, n_grp):
+        pl.semaphore_signal(
+            barrier, inc=1, device_id={"grp": (g + d) % n_grp}, device_id_type=pl.DeviceIdType.MESH
+        )
+    for d in range(1, blocks):
+        pl.semaphore_signal(
+            barrier, inc=1, device_id={"blk": (b + d) % blocks}, device_id_type=pl.DeviceIdType.MESH
+        )
+    pl.semaphore_wait(barrier, n_grp + blocks - 2)
+
+    for p in range(n_grp):
+        send(g != p, lambda p=p: remote(dm_ref, dm_full.at[g], s_dm.at[p], r_dm.at[g], {"grp": p}))
+    for i, ref in enumerate((q_ref, k_ref, v_ref)):
+        for h in range(HEAD_GRP):
+            tile = (slice(None), slice(h * HD, (h + 1) * HD))
+            send(
+                b != owners[h],
+                lambda i=i, ref=ref, h=h, tile=tile: remote(
+                    ref.at[tile], qkv_in.at[i, b], s_qkv.at[i, h], r_qkv.at[i, b], {"blk": owners[h]}
+                ),
+            )
+
+            @pl.when(b == owners[h])
+            def _(i=i, ref=ref, tile=tile):
+                qkv_in[i, b] = ref[tile]
+
+    for h in range(HEAD_GRP):
+        send(
+            b != owners[h],
+            lambda h=h: remote(
+                slot_ref, slots_in.at[b], s_slot.at[h], r_slot.at[b], {"blk": owners[h]}
+            ),
+        )
+    slots_in[b] = slot_ref[...]
+    dm_full[g] = dm_ref[...]
+
+    for p in range(n_grp):
+        arrive(g != p, lambda p=p: remote(dm_ref, dm_full.at[p], s_dm.at[p], r_dm.at[p], {"grp": p}))
+    d_proj = jnp.zeros((rows, HEAD_GRP * HD), F32)
+    for p in range(n_grp):
+        d_proj = d_proj + dot(dm_full[p], w_ref[:, p * feat : (p + 1) * feat], 1, 1)
+    d_proj = d_proj.astype(BF16)
+    for h in range(HEAD_GRP):
+        dp_send[h] = d_proj[:, h * HD : (h + 1) * HD]
+        send(
+            b != owners[h],
+            lambda h=h: remote(
+                dp_send.at[h], do_in.at[b], s_do.at[h], r_do.at[b], {"blk": owners[h]}
+            ),
+        )
+
+        @pl.when(b == owners[h])
+        def _(h=h):
+            do_in[b] = dp_send[h]
+
+    my_rows = pl.ds(pl.multiple_of(g * quarter, quarter), quarter)
+    for t in range(blocks):
+        lo = t * cols
+        view = (lo // feat, my_rows, slice(lo % feat, lo % feat + cols))
+        send(
+            b != t,
+            lambda t=t, view=view: remote(
+                dm_full.at[view], d_cols.at[g, b], s_ca.at[t], r_ca.at[b], {"blk": t}
+            ),
+        )
+
+        @pl.when(b == t)
+        def _(view=view):
+            d_cols[g, b] = dm_full[view]
+
+    @pl.when(is_owner)
+    def _():
+        for t in range(blocks):
+
+            @pl.when(b != t)
+            def _(t=t):
+                remote(slot_ref, slots_in.at[t], s_slot.at[0], r_slot.at[t], {"blk": t}).wait_recv()
+                for i in range(3):
+                    remote(
+                        qkv_in.at[i, t], qkv_in.at[i, t], s_qkv.at[i, 0], r_qkv.at[i, t], {"blk": t}
+                    ).wait_recv()
+
+        slot_row = jnp.concatenate([slots_in[t] for t in range(blocks)], axis=1)
+
+        def forward(i, carry):
+            qc = qkv_in[0, pl.ds(i * per, per)].reshape(step, HD)
+            raw = dot(qc, qkv_in[1].reshape(seq, HD), 1, 1)
+            peak = jnp.max(raw, axis=1, keepdims=True)
+            e = jnp.exp2((raw - peak) * (scale * math.log2(math.e)))
+            p = (e * (1.0 / jnp.sum(e, axis=1, keepdims=True))).astype(BF16)
+            probs[i] = p
+            att_ctrl[i] = dot(p, qkv_in[2].reshape(seq, HD), 1, 0).astype(BF16)
+            at = lax.broadcasted_iota(jnp.int32, (step, seq), 0) + i * step
+            place[i] = jnp.where(at == slot_row, 1.0, 0.0).astype(BF16)
+            return carry
+
+        lax.fori_loop(0, chunks, forward, 0)
+        att_main = dot(place[...].reshape(seq, seq), att_ctrl[...].reshape(seq, HD), 0, 0)
+        att_send[...] = att_main.astype(BF16).reshape(blocks, rows, HD)
+        att_all[b, mine] = att_send[b]
+
+    for t in range(blocks):
+        send(
+            is_owner & (b != t),
+            lambda t=t: remote(
+                att_send.at[t], att_all.at[t, mine], s_at.at[t], r_at.at[mine], {"blk": t}
+            ),
+        )
+
+    for t in range(blocks):
+        arrive(
+            b != t,
+            lambda t=t: remote(
+                d_cols.at[g, t], d_cols.at[g, t], s_ca.at[t], r_ca.at[t], {"blk": t}
+            ),
+        )
+    for p in range(n_grp):
+        send(
+            g != p,
+            lambda p=p: remote(d_cols.at[g], d_cols.at[g], s_cb.at[p], r_cb.at[g], {"grp": p}),
+        )
+
+    for h in range(HEAD_GRP):
+        arrive(
+            b != owners[h],
+            lambda h=h: remote(
+                att_all.at[b, h], att_all.at[b, h], s_at.at[0], r_at.at[h], {"blk": owners[h]}
+            ),
+        )
+
+    def pass_on(cond, slot, dev, sem):
+        send(
+            cond,
+            lambda: remote(att_all.at[slot], att_all.at[slot], s_ag.at[sem], r_ag.at[slot], {"blk": dev}),
+        )
+
+    def landed(cond, slot):
+        arrive(
+            cond,
+            lambda: remote(att_all.at[slot], att_all.at[slot], s_ag.at[0], r_ag.at[slot], {"blk": mate}),
+        )
+
+    always = b >= 0
+    pass_on(z < nz - 1, b, b + 2, 0)
+    pass_on(z > 0, b, b - 2, 1)
+    pass_on(always, b, mate, 2)
+
+    def gather_step(s):
+        if s >= nz:
+            return
+        low, high = z >= s, z + s < nz
+        landed(low, b - 2 * s)
+        pass_on(low & (z < nz - 1), b - 2 * s, b + 2, 4 * s)
+        pass_on(low, b - 2 * s, mate, 4 * s + 1)
+        landed(high, b + 2 * s)
+        pass_on(high & (z > 0), b + 2 * s, b - 2, 4 * s + 2)
+        pass_on(high, b + 2 * s, mate, 4 * s + 3)
+
+    own = jnp.concatenate([att_all[b, h] for h in range(HEAD_GRP)], axis=1)
+    for p in range(n_grp):
+        rs_send[p] = dot(own, w_ref[:, p * feat : (p + 1) * feat], 1, 0).astype(BF16)
+        send(g != p, lambda p=p: remote(rs_send.at[p], rs_in.at[g], s_rs.at[p], r_rs.at[g], {"grp": p}))
+    rs_in[g] = rs_send[g]
+
+    for i in range(chunks):
+
+        @pl.when(is_owner)
+        def _(i=i):
+            if i == 0:
+                for t in range(blocks):
+
+                    @pl.when(b != t)
+                    def _(t=t):
+                        remote(
+                            do_in.at[t], do_in.at[t], s_do.at[0], r_do.at[t], {"blk": t}
+                        ).wait_recv()
+
+            do = dot(place[i], do_in[...].reshape(seq, HD), 1, 0)
+            delta = jnp.sum(do * att_ctrl[i].astype(F32), axis=1, keepdims=True)
+            do = do.astype(BF16)
+            p = probs[i]
+            d_probs = dot(do, qkv_in[2].reshape(seq, HD), 1, 1)
+            ds = (p.astype(F32) * (d_probs - delta)).astype(BF16)
+            dq = (dot(ds, qkv_in[1].reshape(seq, HD), 1, 0) * scale).astype(BF16)
+            grad_send[0, pl.ds(i * per, per)] = dq.reshape(per, rows, HD)
+            qc = qkv_in[0, pl.ds(i * per, per)].reshape(step, HD)
+            dk = dot(ds, qc, 0, 0)
+            dv = dot(p, do, 0, 0)
+            if i == 0:
+                dk_acc[...] = dk
+                dv_acc[...] = dv
+            elif i < chunks - 1:
+                dk_acc[...] += dk
+                dv_acc[...] += dv
+            else:
+                dk = ((dk_acc[...] + dk) * scale).astype(BF16)
+                grad_send[1] = dk.reshape(blocks, rows, HD)
+                grad_send[2] = (dv_acc[...] + dv).astype(BF16).reshape(blocks, rows, HD)
+
+        for t in range(i * per, (i + 1) * per):
+            send(
+                is_owner & (b != t),
+                lambda t=t: remote(
+                    grad_send.at[0, t], grad_in.at[0, mine], s_gr.at[0, t], r_gr.at[0, mine], {"blk": t}
+                ),
+            )
+        if i == chunks - 1:
+            for n in (1, 2):
+                for t in range(blocks):
+                    send(
+                        is_owner & (b != t),
+                        lambda n=n, t=t: remote(
+                            grad_send.at[n, t], grad_in.at[n, mine], s_gr.at[n, t],
+                            r_gr.at[n, mine], {"blk": t},
+                        ),
+                    )
+        gather_step(i + 1)
+
+    @pl.when(is_owner)
+    def _():
+        for n in range(3):
+            grad_in[n, mine] = grad_send[n, b]
+
+    for p in range(n_grp):
+        arrive(g != p, lambda p=p: remote(rs_in.at[p], rs_in.at[p], s_rs.at[p], r_rs.at[p], {"grp": p}))
+    total = rs_in[0].astype(F32)
+    for p in range(1, n_grp):
+        total = total + rs_in[p].astype(F32)
+    mixed_ref[...] = (hidden_ref[...].astype(F32) + total).astype(BF16)
+
+    for p in range(n_grp):
+        arrive(g != p, lambda p=p: remote(d_cols.at[p], d_cols.at[p], s_cb.at[p], r_cb.at[p], {"grp": p}))
+    for j in range(nz):
+        landed(always, 2 * j + 1 - x)
+    grads = d_cols[...].reshape(seq, cols)
+    for h in range(HEAD_GRP):
+        att = jnp.concatenate(
+            [
+                att_all[:, h, p * quarter : (p + 1) * quarter, :].reshape(blocks * quarter, HD)
+                for p in range(n_grp)
+            ],
+            axis=0,
+        )
+        dw_ref[h * HD : (h + 1) * HD, :] = dot(att, grads, 0, 0)
+
+    for n, out in enumerate((dq_ref, dk_ref, dv_ref)):
+        for h in range(HEAD_GRP):
+            arrive(
+                b != owners[h],
+                lambda n=n, h=h: remote(
+                    grad_in.at[n, h], grad_in.at[n, h], s_gr.at[n, 0], r_gr.at[n, h], {"blk": owners[h]}
+                ),
+            )
+            out[:, h * HD : (h + 1) * HD] = grad_in[n, h]
+
+    for cond, make in pending:
+        pl.when(cond)(lambda make=make: make().wait_send())
+
+
+def on_device_fused(main_hidden, ctrl_query, ctrl_key, ctrl_value, w_out, d_mixed, control_slot):
+    n_grp, blocks = lax.axis_size("grp"), lax.axis_size("blk")
+    rows, feat = d_mixed.shape
+    width, model = w_out.shape
+    cols = model // blocks
+    seq = rows * blocks
+    step = seq // 4
+    dma = pltpu.SemaphoreType.DMA
+    sems = [
+        dma((n_grp,)), dma((3, HEAD_GRP)), dma((HEAD_GRP,)), dma((HEAD_GRP,)), dma((blocks,)),
+        dma((n_grp,)), dma((blocks,)), dma((2 * blocks,)), dma((n_grp,)), dma((3, blocks)),
+        dma((n_grp,)), dma((3, blocks)), dma((blocks,)), dma((blocks,)), dma((blocks,)),
+        dma((n_grp,)), dma((HEAD_GRP,)), dma((blocks,)), dma((n_grp,)), dma((3, HEAD_GRP)),
+    ]
+    vmem = pl.BlockSpec(memory_space=pltpu.VMEM)
+    tile = jax.ShapeDtypeStruct((rows, width), BF16)
+    return pl.pallas_call(
+        fused_kernel,
+        out_shape=(
+            jax.ShapeDtypeStruct((rows, feat), BF16), tile, tile, tile,
+            jax.ShapeDtypeStruct((width, cols), F32),
+        ),
+        in_specs=[vmem] * 7,
+        out_specs=[vmem] * 5,
+        scratch_shapes=[
+            pltpu.VMEM((n_grp, rows, feat), BF16),
+            pltpu.VMEM((3, blocks, rows, HD), BF16),
+            pltpu.VMEM((blocks, 1, rows), jnp.int32),
+            pltpu.VMEM((HEAD_GRP, rows, HD), BF16),
+            pltpu.VMEM((blocks, rows, HD), BF16),
+            pltpu.VMEM((blocks, rows, HD), BF16),
+            pltpu.VMEM((n_grp, blocks, rows // n_grp, cols), BF16),
+            pltpu.VMEM((4, step, seq), BF16),
+            pltpu.VMEM((4, step, seq), BF16),
+            pltpu.VMEM((4, step, HD), BF16),
+            pltpu.VMEM((blocks, rows, HD), BF16),
+            pltpu.VMEM((blocks, HEAD_GRP, rows, HD), BF16),
+            pltpu.VMEM((n_grp, rows, feat), BF16),
+            pltpu.VMEM((n_grp, rows, feat), BF16),
+            pltpu.VMEM((seq, HD), F32),
+            pltpu.VMEM((seq, HD), F32),
+            pltpu.VMEM((3, blocks, rows, HD), BF16),
+            pltpu.VMEM((3, HEAD_GRP, rows, HD), BF16),
+        ] + sems,
+        compiler_params=pltpu.CompilerParams(
+            collective_id=0, has_side_effects=True, vmem_limit_bytes=48 * 2**20
+        ),
+        cost_estimate=pl.CostEstimate(
+            flops=2 * 5 * seq * seq * HD, bytes_accessed=16 * 2**20, transcendentals=seq * seq
+        ),
+    )(
+        main_hidden, ctrl_query, ctrl_key, ctrl_value, w_out, d_mixed,
+        control_slot.reshape(1, rows),
+    )
+
+
 def solution(mesh):
     in_specs = (
         P("blk", "grp"),
@@ -165,6 +533,7 @@
         P("blk", "grp"),
         P("grp", "blk"),
     )
+    body = on_device_fused if mesh.shape["blk"] == 8 else on_device
     return jax.shard_map(
-        on_device, mesh=mesh, in_specs=in_specs, out_specs=out_specs, check_vma=False
-    )
+        body, mesh=mesh, in_specs=in_specs, out_specs=out_specs, check_vma=False
+    )

time: 285 us -> 57.7 us (0.20)
  blocking collectives: 192 us -> 0 us
  Pallas kernels: 0 us -> 46.5 us
  matrix products: 29.2 us -> 0 us
  between operations: 14.4 us -> 0.66 us
  waiting for transfers between devices: 13.2 us -> 0 us
  starting transfers between devices: 12.5 us -> 0 us
  other arithmetic: 10.4 us -> 0 us
    all_gather x7 -> x0, blocking collectives: 192 us -> none  [the longest x1 34.2 us: on_device(): lax.all_gather(ctrl_key, 'blk', axis=0, tiled=True)]
    pallas_call x0 -> x1, Pallas kernels: none -> 46.5 us  [on_device_fused(): pl.pallas_call(fused_kernel, out_shape=(jax.ShapeDtypeStruct((rows, feat)...]
    dot_general x21 -> x0, matrix products: 29.2 us -> none  [the longest x3 6.8 us: on_device(): jnp.dot(d_scores.T, query_piece[:, columns], preferred_element_type=jnp.f...]
    all_to_all x3 -> x0, waiting for transfers between devices: 13.2 us -> none  [the longest x1 6.4 us: on_device(): lax.all_to_all(d_mixed[sort_order].reshape(blocks, per_peer, feature_cols...]
    all_to_all x3 -> x0, starting transfers between devices: 12.4 us -> none  [the longest x1 5.53 us: on_device(): lax.all_to_all(send_within, 'blk', split_axis=0, concat_axis=0, tiled=True)]
    unnamed x39 -> x19, local copies, waits for them, and re-layouts: 5.04 us -> 10.3 us
    gather x4 -> x0, local copies, waits for them, and re-layouts: 5.16 us -> none  [the longest x1 1.57 us: on_device(): residual[placed].reshape(blocks, per_peer, feature_cols)]
    sort x2 -> x0, other arithmetic: 5.07 us -> none  [the longest x1 2.54 us: on_device(): sort_order = jnp.argsort(target)]
  transfers between devices with their start and end apart: 5 -> 0, of which waited for: 3 -> 0; matrix products, arithmetic and copies ran while one was open for 16% -> 0% of each run, Pallas kernels for 0% -> 0%
where the time goes in v2:
time: 57.7 us; the launch traced here: 57.4 us
  Pallas kernels  46.5 us (81%)
  local copies, waits for them, and re-layouts  10.3 us (18%)
  between operations  0.66 us (1%)
    pallas_call x1, Pallas kernels, on_device_fused(): pl.pallas_call(fused_kernel, out_shape=(jax.ShapeDtypeStruct((rows, feat)...  46.5 us
    unnamed x19, local copies, waits for them, and re-layouts  10.3 us

profile of v2, /device:TPU:0, one launch (start us, length us, event | category | flops | bytes accessed | tf_op | source)
XLA Modules:
  0.0 57.4 jit_solution(9761764511618309282)
XLA Ops:
  0.6 0.0 copy-start
  0.6 1.7 %copy-done = bf16[384,3072]{1,0:T(8,128)(2,1)S(1)} copy-done((bf16[384,3072]{1,0:T(8,128)(2,1)S(1)}, bf16[384,3072]{1,0:T(8,128)(2,1)}, u32[]{:S(2)}) %copy-start) | copy-done | bytes 2359320
  2.3 0.0 copy-start.1
  2.3 0.9 %copy-done.1 = bf16[128,768]{1,0:T(8,128)(2,1)S(1)} copy-done((bf16[128,768]{1,0:T(8,128)(2,1)S(1)}, bf16[128,768]{1,0:T(8,128)(2,1)}, u32[]{:S(2)}) %copy-start.1) | copy-done | bytes 196632
  3.2 0.0 copy-start.2
  3.2 0.9 %copy-done.2 = bf16[128,768]{1,0:T(8,128)(2,1)S(1)} copy-done((bf16[128,768]{1,0:T(8,128)(2,1)S(1)}, bf16[128,768]{1,0:T(8,128)(2,1)}, u32[]{:S(2)}) %copy-start.2) | copy-done | bytes 196632
  4.2 0.0 copy-start.3
  4.2 0.9 %copy-done.3 = bf16[128,384]{1,0:T(8,128)(2,1)S(1)} copy-done((bf16[128,384]{1,0:T(8,128)(2,1)S(1)}, bf16[128,384]{1,0:T(8,128)(2,1)}, u32[]{:S(2)}) %copy-start.3) | copy-done | bytes 98328
  5.0 0.0 copy-start.4
  5.0 0.9 %copy-done.4 = bf16[128,384]{1,0:T(8,128)(2,1)S(1)} copy-done((bf16[128,384]{1,0:T(8,128)(2,1)S(1)}, bf16[128,384]{1,0:T(8,128)(2,1)}, u32[]{:S(2)}) %copy-start.4) | copy-done | bytes 98328
  5.9 0.0 copy-start.5
  5.9 0.9 %copy-done.5 = bf16[128,384]{1,0:T(8,128)(2,1)S(1)} copy-done((bf16[128,384]{1,0:T(8,128)(2,1)S(1)}, bf16[128,384]{1,0:T(8,128)(2,1)}, u32[]{:S(2)}) %copy-start.5) | copy-done | bytes 98328
  6.8 0.0 copy-start.6
  6.8 0.7 %copy-done.6 = s32[128]{0:T(128)S(1)} copy-done((s32[128]{0:T(128)S(1)}, s32[128]{0:T(128)}, u32[]{:S(2)}) %copy-start.6) | copy-done | bytes 536
  7.5 46.5 %shard_map.110 = (bf16[128,768]{1,0:T(8,128)(2,1)S(1)}, bf16[128,384]{1,0:T(8,128)(2,1)S(1)}, bf16[128,384]{1,0:T(8,128)(2,1)S(1)}, bf16[128,384]{1,0:T(8,128)(2,1)S(1)}, f32[384,384]{1,0:T(8,128)S(1)}) custom-call(bf16[128,768]{1,0:T(8,128)(2,1)S(1)} %copy-done.1, bf16[128,384]{1,0:T(8,128)(2,1)S(1)} %copy-done.3, bf16[128,384]{1,0:T(8,128)(2,1)S(1)} %copy-done.4, ...), custom_call_target="tpu_custom_call" | custom-call | flops 1342177280 | bytes 16777216 | tf_op jit(solution)/shard_map/pallas_call | solution.py:479
  54.0 0.7 %copy.17 = bf16[128,768]{1,0:T(8,128)(2,1)} copy(bf16[128,768]{1,0:T(8,128)(2,1)S(1)} %get-tuple-element.10) | data formatting | bytes 393216
  54.7 0.6 %copy.18 = bf16[128,384]{1,0:T(8,128)(2,1)} copy(bf16[128,384]{1,0:T(8,128)(2,1)S(1)} %get-tuple-element.11) | data formatting | bytes 196608
  55.3 0.6 %copy.19 = bf16[128,384]{1,0:T(8,128)(2,1)} copy(bf16[128,384]{1,0:T(8,128)(2,1)S(1)} %get-tuple-element.12) | data formatting | bytes 196608
  56.0 0.6 %copy.20 = bf16[128,384]{1,0:T(8,128)(2,1)} copy(bf16[128,384]{1,0:T(8,128)(2,1)S(1)} %get-tuple-element.13) | data formatting | bytes 196608
  56.6 0.8 %copy.21 = f32[384,384]{1,0:T(8,128)} copy(f32[384,384]{1,0:T(8,128)S(1)} %get-tuple-element.14) | data formatting | bytes 1179648
Async XLA Ops:
  0.6 1.7 %copy-start = (bf16[384,3072]{1,0:T(8,128)(2,1)S(1)}, bf16[384,3072]{1,0:T(8,128)(2,1)}, u32[]{:S(2)}) copy-start(bf16[384,3072]{1,0:T(8,128)(2,1)} %w_ref.1) | copy-start | bytes 7077892
  2.3 0.9 %copy-start.1 = (bf16[128,768]{1,0:T(8,128)(2,1)S(1)}, bf16[128,768]{1,0:T(8,128)(2,1)}, u32[]{:S(2)}) copy-start(bf16[128,768]{1,0:T(8,128)(2,1)} %hidden_ref.1) | copy-start | bytes 589828
  3.2 0.9 %copy-start.2 = (bf16[128,768]{1,0:T(8,128)(2,1)S(1)}, bf16[128,768]{1,0:T(8,128)(2,1)}, u32[]{:S(2)}) copy-start(bf16[128,768]{1,0:T(8,128)(2,1)} %dm_ref.1) | copy-start | bytes 589828
  4.2 0.9 %copy-start.3 = (bf16[128,384]{1,0:T(8,128)(2,1)S(1)}, bf16[128,384]{1,0:T(8,128)(2,1)}, u32[]{:S(2)}) copy-start(bf16[128,384]{1,0:T(8,128)(2,1)} %q_ref.1) | copy-start | bytes 294916
  5.0 0.9 %copy-start.4 = (bf16[128,384]{1,0:T(8,128)(2,1)S(1)}, bf16[128,384]{1,0:T(8,128)(2,1)}, u32[]{:S(2)}) copy-start(bf16[128,384]{1,0:T(8,128)(2,1)} %k_ref.1) | copy-start | bytes 294916
  5.9 0.9 %copy-start.5 = (bf16[128,384]{1,0:T(8,128)(2,1)S(1)}, bf16[128,384]{1,0:T(8,128)(2,1)}, u32[]{:S(2)}) copy-start(bf16[128,384]{1,0:T(8,128)(2,1)} %v_ref.1) | copy-start | bytes 294916
  6.8 0.7 %copy-start.6 = (s32[128]{0:T(128)S(1)}, s32[128]{0:T(128)}, u32[]{:S(2)}) copy-start(s32[128]{0:T(128)} %param.13) | copy-start | bytes 1540

commit v3 on v2

--- a/solution.py
+++ b/solution.py
@@ -159,12 +159,12 @@
 
 
 def fused_kernel(
-    hidden_ref, q_ref, k_ref, v_ref, w_ref, dm_ref, slot_ref,
-    mixed_ref, dq_ref, dk_ref, dv_ref, dw_ref,
+    hidden_hbm, q_ref, k_ref, v_ref, w_hbm, dm_ref, slot_ref,
+    mixed_out, dq_out, dk_out, dv_out, dw_out, mixed_ref, dw_ref, hidden_ref, w_ref,
     dm_full, qkv_in, slots_in, dp_send, do_in, do_ctrl, d_cols,
     probs, place, att_ctrl, att_send, att_all, rs_send, rs_in,
     dk_acc, dv_acc, grad_send, grad_in,
-    s_dm, s_qkv, s_slot, s_do, s_ca, s_cb, s_at, s_ag, s_rs, s_gr,
+    s_dm, s_qkv, s_slot, s_do, s_ca, s_cb, s_at, s_ag, s_rs, s_gr, s_in, s_out,
     r_dm, r_qkv, r_slot, r_do, r_ca, r_cb, r_at, r_ag, r_rs, r_gr,
 ):
     g = lax.axis_index("grp")
@@ -186,6 +186,12 @@
     mine = jnp.where(b == owners[1], 1, jnp.where(b == owners[2], 2, 0))
     is_owner = (b == owners[0]) | (b == owners[1]) | (b == owners[2])
     pending = []
+    writes = []
+
+    def write(src, dst):
+        copy = pltpu.make_async_copy(src, dst, s_out.at[len(writes)])
+        copy.start()
+        writes.append(copy)
 
     def remote(src, dst, ss, rs, dev):
         return pltpu.make_async_remote_copy(
@@ -199,6 +205,18 @@
 
     def arrive(cond, make):
         pl.when(cond)(lambda: make().wait_recv())
+
+    loads = [
+        pltpu.make_async_copy(dm_ref, dm_full.at[g], s_in.at[0]),
+        pltpu.make_async_copy(w_hbm, w_ref, s_in.at[1]),
+        pltpu.make_async_copy(slot_ref, slots_in.at[b], s_in.at[2]),
+        pltpu.make_async_copy(hidden_hbm, hidden_ref, s_in.at[3]),
+    ]
+    for load in loads:
+        load.start()
+
+    def own_tile(i, ref, tile):
+        return pltpu.make_async_copy(ref.at[tile], qkv_in.at[i, b], s_in.at[4 + i])
 
     barrier = pltpu.get_barrier_semaphore()
     for d in range(1, n_grp):
@@ -225,7 +243,7 @@
 
             @pl.when(b == owners[h])
             def _(i=i, ref=ref, tile=tile):
-                qkv_in[i, b] = ref[tile]
+                own_tile(i, ref, tile).start()
 
     for h in range(HEAD_GRP):
         send(
@@ -234,11 +252,11 @@
                 slot_ref, slots_in.at[b], s_slot.at[h], r_slot.at[b], {"blk": owners[h]}
             ),
         )
-    slots_in[b] = slot_ref[...]
-    dm_full[g] = dm_ref[...]
 
     for p in range(n_grp):
         arrive(g != p, lambda p=p: remote(dm_ref, dm_full.at[p], s_dm.at[p], r_dm.at[p], {"grp": p}))
+    loads[0].wait()
+    loads[1].wait()
     d_proj = jnp.zeros((rows, HEAD_GRP * HD), F32)
     for p in range(n_grp):
         d_proj = d_proj + dot(dm_full[p], w_ref[:, p * feat : (p + 1) * feat], 1, 1)
@@ -271,6 +289,8 @@
         def _(view=view):
             d_cols[g, b] = dm_full[view]
 
+    loads[2].wait()
+
     @pl.when(is_owner)
     def _():
         for t in range(blocks):
@@ -282,6 +302,9 @@
                     remote(
                         qkv_in.at[i, t], qkv_in.at[i, t], s_qkv.at[i, 0], r_qkv.at[i, t], {"blk": t}
                     ).wait_recv()
+
+        for i, ref in enumerate((q_ref, k_ref, v_ref)):
+            own_tile(i, ref, (slice(None), slice(0, HD))).wait()
 
         slot_row = jnp.concatenate([slots_in[t] for t in range(blocks)], axis=1)
 
@@ -426,10 +449,12 @@
 
     for p in range(n_grp):
         arrive(g != p, lambda p=p: remote(rs_in.at[p], rs_in.at[p], s_rs.at[p], r_rs.at[p], {"grp": p}))
+    loads[3].wait()
     total = rs_in[0].astype(F32)
     for p in range(1, n_grp):
         total = total + rs_in[p].astype(F32)
     mixed_ref[...] = (hidden_ref[...].astype(F32) + total).astype(BF16)
+    write(mixed_ref, mixed_out)
 
     for p in range(n_grp):
         arrive(g != p, lambda p=p: remote(d_cols.at[p], d_cols.at[p], s_cb.at[p], r_cb.at[p], {"grp": p}))
@@ -444,9 +469,10 @@
             ],
             axis=0,
         )
-        dw_ref[h * HD : (h + 1) * HD, :] = dot(att, grads, 0, 0)
-
-    for n, out in enumerate((dq_ref, dk_ref, dv_ref)):
+        dw_ref[h] = dot(att, grads, 0, 0)
+        write(dw_ref.at[h], dw_out.at[h * HD : (h + 1) * HD])
+
+    for n, out in enumerate((dq_out, dk_out, dv_out)):
         for h in range(HEAD_GRP):
             arrive(
                 b != owners[h],
@@ -454,10 +480,21 @@
                     grad_in.at[n, h], grad_in.at[n, h], s_gr.at[n, 0], r_gr.at[n, h], {"blk": owners[h]}
                 ),
             )
-            out[:, h * HD : (h + 1) * HD] = grad_in[n, h]
-
+            write(grad_in.at[n, h], out.at[:, h * HD : (h + 1) * HD])
+
+    for copy in writes:
+        copy.wait()
     for cond, make in pending:
         pl.when(cond)(lambda make=make: make().wait_send())
+
+
+def write_kernel(*refs):
+    sems = refs[10]
+    copies = [pltpu.make_async_copy(refs[i], refs[5 + i], sems.at[i]) for i in range(5)]
+    for copy in copies:
+        copy.start()
+    for copy in copies:
+        copy.wait()
 
 
 def on_device_fused(main_hidden, ctrl_query, ctrl_key, ctrl_value, w_out, d_mixed, control_slot):
@@ -470,21 +507,25 @@
     dma = pltpu.SemaphoreType.DMA
     sems = [
         dma((n_grp,)), dma((3, HEAD_GRP)), dma((HEAD_GRP,)), dma((HEAD_GRP,)), dma((blocks,)),
-        dma((n_grp,)), dma((blocks,)), dma((2 * blocks,)), dma((n_grp,)), dma((3, blocks)),
+        dma((n_grp,)), dma((blocks,)), dma((2 * blocks,)), dma((n_grp,)), dma((3, blocks)), dma((7,)), dma((16,)),
         dma((n_grp,)), dma((3, blocks)), dma((blocks,)), dma((blocks,)), dma((blocks,)),
         dma((n_grp,)), dma((HEAD_GRP,)), dma((blocks,)), dma((n_grp,)), dma((3, HEAD_GRP)),
     ]
-    vmem = pl.BlockSpec(memory_space=pltpu.VMEM)
+    hbm = pl.BlockSpec(memory_space=pltpu.HBM)
     tile = jax.ShapeDtypeStruct((rows, width), BF16)
-    return pl.pallas_call(
+    results = pl.pallas_call(
         fused_kernel,
         out_shape=(
             jax.ShapeDtypeStruct((rows, feat), BF16), tile, tile, tile,
             jax.ShapeDtypeStruct((width, cols), F32),
         ),
-        in_specs=[vmem] * 7,
-        out_specs=[vmem] * 5,
+        in_specs=[hbm] * 7,
+        out_specs=[hbm] * 5,
         scratch_shapes=[
+            pltpu.VMEM((rows, feat), BF16),
+            pltpu.VMEM((HEAD_GRP, HD, cols), F32),
+            pltpu.VMEM((rows, feat), BF16),
+            pltpu.VMEM((width, model), BF16),
             pltpu.VMEM((n_grp, rows, feat), BF16),
             pltpu.VMEM((3, blocks, rows, HD), BF16),
             pltpu.VMEM((blocks, 1, rows), jnp.int32),
@@ -505,7 +546,7 @@
             pltpu.VMEM((3, HEAD_GRP, rows, HD), BF16),
         ] + sems,
         compiler_params=pltpu.CompilerParams(
-            collective_id=0, has_side_effects=True, vmem_limit_bytes=48 * 2**20
+            collective_id=0, has_side_effects=True, vmem_limit_bytes=60 * 2**20
         ),
         cost_estimate=pl.CostEstimate(
             flops=2 * 5 * seq * seq * HD, bytes_accessed=16 * 2**20, transcendentals=seq * seq
@@ -514,6 +555,14 @@
         main_hidden, ctrl_query, ctrl_key, ctrl_value, w_out, d_mixed,
         control_slot.reshape(1, rows),
     )
+    return pl.pallas_call(
+        write_kernel,
+        out_shape=tuple(jax.ShapeDtypeStruct(r.shape, r.dtype) for r in results),
+        in_specs=[hbm] * 5,
+        out_specs=[hbm] * 5,
+        scratch_shapes=[dma((5,))],
+        compiler_params=pltpu.CompilerParams(vmem_limit_bytes=60 * 2**20),
+    )(*results)
 
 
 def solution(mesh):

time: 57.7 us -> 82.5 us (1.43)
  Pallas kernels: 46.5 us -> 81.7 us
  local copies, waits for them, and re-layouts: 10.3 us -> 0 us
    pallas_call x0 -> x1, Pallas kernels: none -> 33.9 us  [on_device_fused(): pl.pallas_call(write_kernel, out_shape=tuple((jax.ShapeDtypeStruct(r.shap...]
    unnamed x19 -> x0, local copies, waits for them, and re-layouts: 10.3 us -> none
    pallas_call x1, Pallas kernels: 46.5 us -> 47.8 us  [on_device_fused(): pl.pallas_call(fused_kernel, out_shape=(jax.ShapeDtypeStruct((rows, feat)...]
where the time goes in v3:
time: 82.5 us; the launch traced here: 82.3 us
  Pallas kernels  81.7 us (99%)
    pallas_call x1, Pallas kernels, on_device_fused(): pl.pallas_call(fused_kernel, out_shape=(jax.ShapeDtypeStruct((rows, feat)...  47.8 us
    pallas_call x1, Pallas kernels, on_device_fused(): pl.pallas_call(write_kernel, out_shape=tuple((jax.ShapeDtypeStruct(r.shap...  33.9 us

profile of v3, /device:TPU:0, one launch (start us, length us, event | category | flops | bytes accessed | tf_op | source)
XLA Modules:
  0.0 82.3 jit_solution(14903845311912480535)
XLA Ops:
  0.6 47.8 %shard_map.110 = (bf16[128,768]{1,0:T(8,128)(2,1)}, bf16[128,384]{1,0:T(8,128)(2,1)}, bf16[128,384]{1,0:T(8,128)(2,1)}, bf16[128,384]{1,0:T(8,128)(2,1)}, f32[384,384]{1,0:T(8,128)}) custom-call(bf16[128,768]{1,0:T(8,128)(2,1)} %hidden_hbm.1, bf16[128,384]{1,0:T(8,128)(2,1)} %q_ref.1, bf16[128,384]{1,0:T(8,128)(2,1)} %k_ref.1, bf16[128,384]{1,0:T(8,128)(2,1)} %v_ref.1, ...), custom_call_target="tpu_custom_call" | custom-call | flops 1342177280 | bytes 16777216 | tf_op jit(solution)/shard_map/pallas_call | solution.py:516
  48.4 33.9 %shard_map.111 = (bf16[128,768]{1,0:T(8,128)(2,1)}, bf16[128,384]{1,0:T(8,128)(2,1)}, bf16[128,384]{1,0:T(8,128)(2,1)}, bf16[128,384]{1,0:T(8,128)(2,1)}, f32[384,384]{1,0:T(8,128)}) custom-call(bf16[128,768]{1,0:T(8,128)(2,1)} %get-tuple-element.10.refs_0_, bf16[128,384]{1,0:T(8,128)(2,1)} %get-tuple-element.11.refs_1_, ...), custom_call_target="tpu_custom_call" | custom-call | tf_op jit(solution)/shard_map/pallas_call | solution.py:558

commit v4 on v3

--- a/solution.py
+++ b/solution.py
@@ -161,8 +161,8 @@
 def fused_kernel(
     hidden_hbm, q_ref, k_ref, v_ref, w_hbm, dm_ref, slot_ref,
     mixed_out, dq_out, dk_out, dv_out, dw_out, mixed_ref, dw_ref, hidden_ref, w_ref,
-    dm_full, qkv_in, slots_in, dp_send, do_in, do_ctrl, d_cols,
-    probs, place, att_ctrl, att_send, att_all, rs_send, rs_in,
+    dm_full, qkv_in, slots_in, dp_send, do_in, q_main, d_cols,
+    probs, place, place_t, dq_main, att_send, att_all, rs_send, rs_pass, rs_in,
     dk_acc, dv_acc, grad_send, grad_in,
     s_dm, s_qkv, s_slot, s_do, s_ca, s_cb, s_at, s_ag, s_rs, s_gr, s_in, s_out,
     r_dm, r_qkv, r_slot, r_do, r_ca, r_cb, r_at, r_ag, r_rs, r_gr,
@@ -182,9 +182,11 @@
     z, x = b // 2, b % 2
     nz = blocks // 2
     mate = b + 1 - 2 * x
+    core_mate, y_mate, diagonal = g + 1 - 2 * c, (g + 2) % n_grp, n_grp - 1 - g
     owners = [2 + 2 * c, 5 - 2 * c, 7 * c]
     mine = jnp.where(b == owners[1], 1, jnp.where(b == owners[2], 2, 0))
     is_owner = (b == owners[0]) | (b == owners[1]) | (b == owners[2])
+    always = b >= 0
     pending = []
     writes = []
 
@@ -229,8 +231,14 @@
         )
     pl.semaphore_wait(barrier, n_grp + blocks - 2)
 
-    for p in range(n_grp):
-        send(g != p, lambda p=p: remote(dm_ref, dm_full.at[g], s_dm.at[p], r_dm.at[g], {"grp": p}))
+    def relay(src, buf, slot, dev, ss, rs):
+        send(always, lambda: remote(src, buf.at[slot], ss, rs.at[slot], {"grp": dev}))
+
+    def relayed(buf, slot, ss, rs):
+        arrive(always, lambda: remote(buf.at[slot], buf.at[slot], ss.at[0], rs.at[slot], {"grp": y_mate}))
+
+    relay(dm_ref, dm_full, g, y_mate, s_dm.at[0], r_dm)
+    relay(dm_ref, dm_full, g, core_mate, s_dm.at[1], r_dm)
     for i, ref in enumerate((q_ref, k_ref, v_ref)):
         for h in range(HEAD_GRP):
             tile = (slice(None), slice(h * HD, (h + 1) * HD))
@@ -253,14 +261,39 @@
             ),
         )
 
-    for p in range(n_grp):
-        arrive(g != p, lambda p=p: remote(dm_ref, dm_full.at[p], s_dm.at[p], r_dm.at[p], {"grp": p}))
+    loads[2].wait()
+
+    @pl.when(is_owner)
+    def _():
+        for t in range(blocks):
+
+            @pl.when(b != t)
+            def _(t=t):
+                remote(slot_ref, slots_in.at[t], s_slot.at[0], r_slot.at[t], {"blk": t}).wait_recv()
+
+        slot_row = jnp.concatenate([slots_in[t] for t in range(blocks)], axis=1)
+        slot_col = jnp.transpose(jnp.broadcast_to(slot_row.astype(F32), (8, seq)))[:, :1]
+        lane = lax.broadcasted_iota(jnp.int32, (step, seq), 1)
+        for i in range(chunks):
+            at = lax.broadcasted_iota(jnp.int32, (step, seq), 0) + i * step
+            place[i] = jnp.where(at == slot_row, 1.0, 0.0).astype(BF16)
+            want = slot_col[i * step : (i + 1) * step].astype(jnp.int32)
+            place_t[i] = jnp.where(lane == want, 1.0, 0.0).astype(BF16)
+
+    def features(p):
+        lo = pl.multiple_of(p * feat, HD)
+        return dot(dm_full[p], w_ref[:, pl.ds(lo, feat)], 1, 1)
+
     loads[0].wait()
     loads[1].wait()
-    d_proj = jnp.zeros((rows, HEAD_GRP * HD), F32)
-    for p in range(n_grp):
-        d_proj = d_proj + dot(dm_full[p], w_ref[:, p * feat : (p + 1) * feat], 1, 1)
-    d_proj = d_proj.astype(BF16)
+    d_proj = features(g)
+    relayed(dm_full, y_mate, s_dm, r_dm)
+    relay(dm_full.at[y_mate], dm_full, y_mate, core_mate, s_dm.at[2], r_dm)
+    d_proj = d_proj + features(y_mate)
+    relayed(dm_full, core_mate, s_dm, r_dm)
+    d_proj = d_proj + features(core_mate)
+    relayed(dm_full, diagonal, s_dm, r_dm)
+    d_proj = (d_proj + features(diagonal)).astype(BF16)
     for h in range(HEAD_GRP):
         dp_send[h] = d_proj[:, h * HD : (h + 1) * HD]
         send(
@@ -289,49 +322,48 @@
         def _(view=view):
             d_cols[g, b] = dm_full[view]
 
-    loads[2].wait()
+    def own_part(i, ref):
+        for t in range(blocks):
+
+            @pl.when(b != t)
+            def _(t=t):
+                remote(
+                    qkv_in.at[i, t], qkv_in.at[i, t], s_qkv.at[i, 0], r_qkv.at[i, t], {"blk": t}
+                ).wait_recv()
+
+        own_tile(i, ref, (slice(None), slice(0, HD))).wait()
 
     @pl.when(is_owner)
     def _():
-        for t in range(blocks):
-
-            @pl.when(b != t)
-            def _(t=t):
-                remote(slot_ref, slots_in.at[t], s_slot.at[0], r_slot.at[t], {"blk": t}).wait_recv()
-                for i in range(3):
-                    remote(
-                        qkv_in.at[i, t], qkv_in.at[i, t], s_qkv.at[i, 0], r_qkv.at[i, t], {"blk": t}
-                    ).wait_recv()
-
-        for i, ref in enumerate((q_ref, k_ref, v_ref)):
-            own_tile(i, ref, (slice(None), slice(0, HD))).wait()
-
-        slot_row = jnp.concatenate([slots_in[t] for t in range(blocks)], axis=1)
-
-        def forward(i, carry):
-            qc = qkv_in[0, pl.ds(i * per, per)].reshape(step, HD)
-            raw = dot(qc, qkv_in[1].reshape(seq, HD), 1, 1)
+        own_part(0, q_ref)
+        for i in range(chunks):
+            q_main[i] = dot(place_t[i], qkv_in[0].reshape(seq, HD), 1, 0).astype(BF16)
+        own_part(1, k_ref)
+        own_part(2, v_ref)
+
+    for i in range(chunks):
+
+        @pl.when(is_owner)
+        def _(i=i):
+            raw = dot(q_main[i], qkv_in[1].reshape(seq, HD), 1, 1)
             peak = jnp.max(raw, axis=1, keepdims=True)
             e = jnp.exp2((raw - peak) * (scale * math.log2(math.e)))
             p = (e * (1.0 / jnp.sum(e, axis=1, keepdims=True))).astype(BF16)
             probs[i] = p
-            att_ctrl[i] = dot(p, qkv_in[2].reshape(seq, HD), 1, 0).astype(BF16)
-            at = lax.broadcasted_iota(jnp.int32, (step, seq), 0) + i * step
-            place[i] = jnp.where(at == slot_row, 1.0, 0.0).astype(BF16)
-            return carry
-
-        lax.fori_loop(0, chunks, forward, 0)
-        att_main = dot(place[...].reshape(seq, seq), att_ctrl[...].reshape(seq, HD), 0, 0)
-        att_send[...] = att_main.astype(BF16).reshape(blocks, rows, HD)
+            att = dot(p, qkv_in[2].reshape(seq, HD), 1, 0).astype(BF16)
+            att_send[i * per : (i + 1) * per] = att.reshape(per, rows, HD)
+
+        for t in range(i * per, (i + 1) * per):
+            send(
+                is_owner & (b != t),
+                lambda t=t: remote(
+                    att_send.at[t], att_all.at[t, mine], s_at.at[t], r_at.at[mine], {"blk": t}
+                ),
+            )
+
+    @pl.when(is_owner)
+    def _():
         att_all[b, mine] = att_send[b]
-
-    for t in range(blocks):
-        send(
-            is_owner & (b != t),
-            lambda t=t: remote(
-                att_send.at[t], att_all.at[t, mine], s_at.at[t], r_at.at[mine], {"blk": t}
-            ),
-        )
 
     for t in range(blocks):
         arrive(
@@ -340,77 +372,26 @@
                 d_cols.at[g, t], d_cols.at[g, t], s_ca.at[t], r_ca.at[t], {"blk": t}
             ),
         )
-    for p in range(n_grp):
-        send(
-            g != p,
-            lambda p=p: remote(d_cols.at[g], d_cols.at[g], s_cb.at[p], r_cb.at[g], {"grp": p}),
-        )
-
-    for h in range(HEAD_GRP):
-        arrive(
-            b != owners[h],
-            lambda h=h: remote(
-                att_all.at[b, h], att_all.at[b, h], s_at.at[0], r_at.at[h], {"blk": owners[h]}
-            ),
-        )
-
-    def pass_on(cond, slot, dev, sem):
-        send(
-            cond,
-            lambda: remote(att_all.at[slot], att_all.at[slot], s_ag.at[sem], r_ag.at[slot], {"blk": dev}),
-        )
-
-    def landed(cond, slot):
-        arrive(
-            cond,
-            lambda: remote(att_all.at[slot], att_all.at[slot], s_ag.at[0], r_ag.at[slot], {"blk": mate}),
-        )
-
-    always = b >= 0
-    pass_on(z < nz - 1, b, b + 2, 0)
-    pass_on(z > 0, b, b - 2, 1)
-    pass_on(always, b, mate, 2)
-
-    def gather_step(s):
-        if s >= nz:
-            return
-        low, high = z >= s, z + s < nz
-        landed(low, b - 2 * s)
-        pass_on(low & (z < nz - 1), b - 2 * s, b + 2, 4 * s)
-        pass_on(low, b - 2 * s, mate, 4 * s + 1)
-        landed(high, b + 2 * s)
-        pass_on(high & (z > 0), b + 2 * s, b - 2, 4 * s + 2)
-        pass_on(high, b + 2 * s, mate, 4 * s + 3)
-
-    own = jnp.concatenate([att_all[b, h] for h in range(HEAD_GRP)], axis=1)
-    for p in range(n_grp):
-        rs_send[p] = dot(own, w_ref[:, p * feat : (p + 1) * feat], 1, 0).astype(BF16)
-        send(g != p, lambda p=p: remote(rs_send.at[p], rs_in.at[g], s_rs.at[p], r_rs.at[g], {"grp": p}))
-    rs_in[g] = rs_send[g]
-
-    for i in range(chunks):
-
+    relay(d_cols.at[g], d_cols, g, y_mate, s_cb.at[0], r_cb)
+    relay(d_cols.at[g], d_cols, g, core_mate, s_cb.at[1], r_cb)
+
+    def backward(i):
         @pl.when(is_owner)
-        def _(i=i):
-            if i == 0:
-                for t in range(blocks):
-
-                    @pl.when(b != t)
-                    def _(t=t):
-                        remote(
-                            do_in.at[t], do_in.at[t], s_do.at[0], r_do.at[t], {"blk": t}
-                        ).wait_recv()
-
-            do = dot(place[i], do_in[...].reshape(seq, HD), 1, 0)
-            delta = jnp.sum(do * att_ctrl[i].astype(F32), axis=1, keepdims=True)
-            do = do.astype(BF16)
+        def _():
+            for t in range(i * per, (i + 1) * per):
+
+                @pl.when(b != t)
+                def _(t=t):
+                    remote(do_in.at[t], do_in.at[t], s_do.at[0], r_do.at[t], {"blk": t}).wait_recv()
+
+            do = do_in[i * per : (i + 1) * per].reshape(step, HD)
+            att = att_send[i * per : (i + 1) * per].reshape(step, HD)
+            delta = jnp.sum(do.astype(F32) * att.astype(F32), axis=1, keepdims=True)
             p = probs[i]
             d_probs = dot(do, qkv_in[2].reshape(seq, HD), 1, 1)
             ds = (p.astype(F32) * (d_probs - delta)).astype(BF16)
-            dq = (dot(ds, qkv_in[1].reshape(seq, HD), 1, 0) * scale).astype(BF16)
-            grad_send[0, pl.ds(i * per, per)] = dq.reshape(per, rows, HD)
-            qc = qkv_in[0, pl.ds(i * per, per)].reshape(step, HD)
-            dk = dot(ds, qc, 0, 0)
+            dq_main[i] = (dot(ds, qkv_in[1].reshape(seq, HD), 1, 0) * scale).astype(BF16)
+            dk = dot(ds, q_main[i], 0, 0)
             dv = dot(p, do, 0, 0)
             if i == 0:
                 dk_acc[...] = dk
@@ -423,41 +404,104 @@
                 grad_send[1] = dk.reshape(blocks, rows, HD)
                 grad_send[2] = (dv_acc[...] + dv).astype(BF16).reshape(blocks, rows, HD)
 
-        for t in range(i * per, (i + 1) * per):
+    def send_grads(n):
+        for t in range(blocks):
             send(
                 is_owner & (b != t),
                 lambda t=t: remote(
-                    grad_send.at[0, t], grad_in.at[0, mine], s_gr.at[0, t], r_gr.at[0, mine], {"blk": t}
+                    grad_send.at[n, t], grad_in.at[n, mine], s_gr.at[n, t], r_gr.at[n, mine], {"blk": t}
                 ),
             )
-        if i == chunks - 1:
-            for n in (1, 2):
-                for t in range(blocks):
-                    send(
-                        is_owner & (b != t),
-                        lambda n=n, t=t: remote(
-                            grad_send.at[n, t], grad_in.at[n, mine], s_gr.at[n, t],
-                            r_gr.at[n, mine], {"blk": t},
-                        ),
-                    )
-        gather_step(i + 1)
+
+    backward(0)
+    for h in range(HEAD_GRP):
+        arrive(
+            b != owners[h],
+            lambda h=h: remote(
+                att_all.at[b, h], att_all.at[b, h], s_at.at[0], r_at.at[h], {"blk": owners[h]}
+            ),
+        )
+
+    def pass_on(cond, slot, dev, sem):
+        send(
+            cond,
+            lambda: remote(att_all.at[slot], att_all.at[slot], s_ag.at[sem], r_ag.at[slot], {"blk": dev}),
+        )
+
+    def landed(cond, slot):
+        arrive(
+            cond,
+            lambda: remote(att_all.at[slot], att_all.at[slot], s_ag.at[0], r_ag.at[slot], {"blk": mate}),
+        )
+
+    pass_on(z < nz - 1, b, b + 2, 0)
+    pass_on(z > 0, b, b - 2, 1)
+    pass_on(always, b, mate, 2)
+
+    def gather_step(s):
+        if s >= nz:
+            return
+        low, high = z >= s, z + s < nz
+        landed(low, b - 2 * s)
+        pass_on(low & (z < nz - 1), b - 2 * s, b + 2, 4 * s)
+        pass_on(low, b - 2 * s, mate, 4 * s + 1)
+        landed(high, b + 2 * s)
+        pass_on(high & (z > 0), b + 2 * s, b - 2, 4 * s + 2)
+        pass_on(high, b + 2 * s, mate, 4 * s + 3)
+
+    backward(1)
+    gather_step(1)
+    relayed(d_cols, y_mate, s_cb, r_cb)
+    relay(d_cols.at[y_mate], d_cols, y_mate, core_mate, s_cb.at[2], r_cb)
+
+    own = jnp.concatenate([att_all[b, h] for h in range(HEAD_GRP)], axis=1)
+    for p in range(n_grp):
+        rs_send[p] = dot(own, w_ref[:, p * feat : (p + 1) * feat], 1, 0).astype(BF16)
+    for n, p in enumerate((diagonal, core_mate)):
+        send(
+            always,
+            lambda n=n, p=p: remote(
+                rs_send.at[p], rs_in.at[n], s_rs.at[n], r_rs.at[n], {"grp": core_mate}
+            ),
+        )
+
+    def rs_landed(n):
+        arrive(always, lambda: remote(rs_in.at[n], rs_in.at[n], s_rs.at[0], r_rs.at[n], {"grp": y_mate}))
+
+    backward(2)
+    gather_step(2)
+    rs_landed(0)
+    rs_pass[...] = (rs_send[y_mate].astype(F32) + rs_in[0].astype(F32)).astype(BF16)
+    send(
+        always,
+        lambda: remote(rs_pass, rs_in.at[2], s_rs.at[2], r_rs.at[2], {"grp": y_mate}),
+    )
+    backward(3)
+    send_grads(1)
+    send_grads(2)
+
+    @pl.when(is_owner)
+    def _():
+        turned = dot(place[...].reshape(seq, seq), dq_main[...].reshape(seq, HD), 1, 0)
+        grad_send[0] = turned.astype(BF16).reshape(blocks, rows, HD)
+
+    send_grads(0)
+    gather_step(3)
 
     @pl.when(is_owner)
     def _():
         for n in range(3):
             grad_in[n, mine] = grad_send[n, b]
 
-    for p in range(n_grp):
-        arrive(g != p, lambda p=p: remote(rs_in.at[p], rs_in.at[p], s_rs.at[p], r_rs.at[p], {"grp": p}))
+    rs_landed(1)
+    rs_landed(2)
     loads[3].wait()
-    total = rs_in[0].astype(F32)
-    for p in range(1, n_grp):
-        total = total + rs_in[p].astype(F32)
+    total = rs_send[g].astype(F32) + rs_in[1].astype(F32) + rs_in[2].astype(F32)
     mixed_ref[...] = (hidden_ref[...].astype(F32) + total).astype(BF16)
     write(mixed_ref, mixed_out)
 
-    for p in range(n_grp):
-        arrive(g != p, lambda p=p: remote(d_cols.at[p], d_cols.at[p], s_cb.at[p], r_cb.at[p], {"grp": p}))
+    relayed(d_cols, core_mate, s_cb, r_cb)
+    relayed(d_cols, diagonal, s_cb, r_cb)
     for j in range(nz):
         landed(always, 2 * j + 1 - x)
     grads = d_cols[...].reshape(seq, cols)
@@ -489,12 +533,16 @@
 
 
 def write_kernel(*refs):
-    sems = refs[10]
-    copies = [pltpu.make_async_copy(refs[i], refs[5 + i], sems.at[i]) for i in range(5)]
-    for copy in copies:
-        copy.start()
-    for copy in copies:
-        copy.wait()
+    srcs, dsts, held, into, out = refs[:5], refs[5:10], refs[10:15], refs[15], refs[16]
+    loads = [pltpu.make_async_copy(srcs[i], held[i], into.at[i]) for i in range(5)]
+    stores = [pltpu.make_async_copy(held[i], dsts[i], out.at[i]) for i in range(5)]
+    for load in loads:
+        load.start()
+    for load, store in zip(loads, stores):
+        load.wait()
+        store.start()
+    for store in stores:
+        store.wait()
 
 
 def on_device_fused(main_hidden, ctrl_query, ctrl_key, ctrl_value, w_out, d_mixed, control_slot):
@@ -531,15 +579,17 @@
             pltpu.VMEM((blocks, 1, rows), jnp.int32),
             pltpu.VMEM((HEAD_GRP, rows, HD), BF16),
             pltpu.VMEM((blocks, rows, HD), BF16),
-            pltpu.VMEM((blocks, rows, HD), BF16),
+            pltpu.VMEM((4, step, HD), BF16),
             pltpu.VMEM((n_grp, blocks, rows // n_grp, cols), BF16),
+            pltpu.VMEM((4, step, seq), BF16),
             pltpu.VMEM((4, step, seq), BF16),
             pltpu.VMEM((4, step, seq), BF16),
             pltpu.VMEM((4, step, HD), BF16),
             pltpu.VMEM((blocks, rows, HD), BF16),
             pltpu.VMEM((blocks, HEAD_GRP, rows, HD), BF16),
             pltpu.VMEM((n_grp, rows, feat), BF16),
-            pltpu.VMEM((n_grp, rows, feat), BF16),
+            pltpu.VMEM((rows, feat), BF16),
+            pltpu.VMEM((3, rows, feat), BF16),
             pltpu.VMEM((seq, HD), F32),
             pltpu.VMEM((seq, HD), F32),
             pltpu.VMEM((3, blocks, rows, HD), BF16),
@@ -560,7 +610,7 @@
         out_shape=tuple(jax.ShapeDtypeStruct(r.shape, r.dtype) for r in results),
         in_specs=[hbm] * 5,
         out_specs=[hbm] * 5,
-        scratch_shapes=[dma((5,))],
+        scratch_shapes=[pltpu.VMEM(r.shape, r.dtype) for r in results] + [dma((5,)), dma((5,))],
         compiler_params=pltpu.CompilerParams(vmem_limit_bytes=60 * 2**20),
     )(*results)
 

time: 82.5 us -> 52.8 us (0.64)
  Pallas kernels: 81.7 us -> 52 us
    pallas_call x1, Pallas kernels: 33.9 us -> 2.22 us  [on_device_fused(): pl.pallas_call(write_kernel, out_shape=tuple((jax.ShapeDtypeStruct(r.shap...]
    pallas_call x1, Pallas kernels: 47.8 us -> 49.7 us  [on_device_fused(): pl.pallas_call(fused_kernel, out_shape=(jax.ShapeDtypeStruct((rows, feat)...]
where the time goes in v4:
time: 52.8 us; the launch traced here: 52.6 us
  Pallas kernels  52 us (98%)
  between operations  0.64 us (1%)
    pallas_call x1, Pallas kernels, on_device_fused(): pl.pallas_call(fused_kernel, out_shape=(jax.ShapeDtypeStruct((rows, feat)...  49.7 us
    pallas_call x1, Pallas kernels, on_device_fused(): pl.pallas_call(write_kernel, out_shape=tuple((jax.ShapeDtypeStruct(r.shap...  2.22 us

profile of v4, /device:TPU:0, one launch (start us, length us, event | category | flops | bytes accessed | tf_op | source)
XLA Modules:
  0.0 52.6 jit_solution(14260741076621327597)
XLA Ops:
  0.6 49.7 %shard_map.110 = (bf16[128,768]{1,0:T(8,128)(2,1)}, bf16[128,384]{1,0:T(8,128)(2,1)}, bf16[128,384]{1,0:T(8,128)(2,1)}, bf16[128,384]{1,0:T(8,128)(2,1)}, f32[384,384]{1,0:T(8,128)}) custom-call(bf16[128,768]{1,0:T(8,128)(2,1)} %hidden_hbm.1, bf16[128,384]{1,0:T(8,128)(2,1)} %q_ref.1, bf16[128,384]{1,0:T(8,128)(2,1)} %k_ref.1, bf16[128,384]{1,0:T(8,128)(2,1)} %v_ref.1, ...), custom_call_target="tpu_custom_call" | custom-call | flops 1342177280 | bytes 16777216 | tf_op jit(solution)/shard_map/pallas_call | solution.py:564
  50.4 2.2 %shard_map.111 = (bf16[128,768]{1,0:T(8,128)(2,1)}, bf16[128,384]{1,0:T(8,128)(2,1)}, bf16[128,384]{1,0:T(8,128)(2,1)}, bf16[128,384]{1,0:T(8,128)(2,1)}, f32[384,384]{1,0:T(8,128)}) custom-call(bf16[128,768]{1,0:T(8,128)(2,1)} %get-tuple-element.10.refs_0_, bf16[128,384]{1,0:T(8,128)(2,1)} %get-tuple-element.11.refs_1_, ...), custom_call_target="tpu_custom_call" | custom-call | tf_op jit(solution)/shard_map/pallas_call | solution.py:608

commit v5 on v4

--- a/solution.py
+++ b/solution.py
@@ -162,7 +162,7 @@
     hidden_hbm, q_ref, k_ref, v_ref, w_hbm, dm_ref, slot_ref,
     mixed_out, dq_out, dk_out, dv_out, dw_out, mixed_ref, dw_ref, hidden_ref, w_ref,
     dm_full, qkv_in, slots_in, dp_send, do_in, q_main, d_cols,
-    probs, place, place_t, dq_main, att_send, att_all, rs_send, rs_pass, rs_in,
+    probs, place, place_t, k_t, v_t, dq_main, att_send, att_all, rs_send, rs_pass, rs_in,
     dk_acc, dv_acc, grad_send, grad_in,
     s_dm, s_qkv, s_slot, s_do, s_ca, s_cb, s_at, s_ag, s_rs, s_gr, s_in, s_out,
     r_dm, r_qkv, r_slot, r_do, r_ca, r_cb, r_at, r_ag, r_rs, r_gr,
@@ -339,19 +339,22 @@
         for i in range(chunks):
             q_main[i] = dot(place_t[i], qkv_in[0].reshape(seq, HD), 1, 0).astype(BF16)
         own_part(1, k_ref)
+        k_t[...] = jnp.transpose(qkv_in[1].reshape(seq, HD).astype(F32)).astype(BF16)
         own_part(2, v_ref)
+        v_t[...] = jnp.transpose(qkv_in[2].reshape(seq, HD).astype(F32)).astype(BF16)
 
     for i in range(chunks):
 
         @pl.when(is_owner)
         def _(i=i):
-            raw = dot(q_main[i], qkv_in[1].reshape(seq, HD), 1, 1)
-            peak = jnp.max(raw, axis=1, keepdims=True)
+            raw = dot(qkv_in[1].reshape(seq, HD), q_main[i], 1, 1)
+            peak = jnp.max(raw, axis=0, keepdims=True)
             e = jnp.exp2((raw - peak) * (scale * math.log2(math.e)))
-            p = (e * (1.0 / jnp.sum(e, axis=1, keepdims=True))).astype(BF16)
+            p = (e * (1.0 / jnp.sum(e, axis=0, keepdims=True))).astype(BF16)
             probs[i] = p
-            att = dot(p, qkv_in[2].reshape(seq, HD), 1, 0).astype(BF16)
-            att_send[i * per : (i + 1) * per] = att.reshape(per, rows, HD)
+            att = dot(v_t[...], p, 1, 0).astype(BF16)
+            for n in range(per):
+                att_send[i * per + n] = att[:, n * rows : (n + 1) * rows]
 
         for t in range(i * per, (i + 1) * per):
             send(
@@ -385,14 +388,22 @@
                     remote(do_in.at[t], do_in.at[t], s_do.at[0], r_do.at[t], {"blk": t}).wait_recv()
 
             do = do_in[i * per : (i + 1) * per].reshape(step, HD)
-            att = att_send[i * per : (i + 1) * per].reshape(step, HD)
-            delta = jnp.sum(do.astype(F32) * att.astype(F32), axis=1, keepdims=True)
+            delta = jnp.concatenate(
+                [
+                    jnp.sum(
+                        jnp.transpose(do_in[t].astype(F32)) * att_send[t].astype(F32),
+                        axis=0, keepdims=True,
+                    )
+                    for t in range(i * per, (i + 1) * per)
+                ],
+                axis=1,
+            )
             p = probs[i]
-            d_probs = dot(do, qkv_in[2].reshape(seq, HD), 1, 1)
+            d_probs = dot(qkv_in[2].reshape(seq, HD), do, 1, 1)
             ds = (p.astype(F32) * (d_probs - delta)).astype(BF16)
-            dq_main[i] = (dot(ds, qkv_in[1].reshape(seq, HD), 1, 0) * scale).astype(BF16)
-            dk = dot(ds, q_main[i], 0, 0)
-            dv = dot(p, do, 0, 0)
+            dq_main[i] = jnp.transpose(dot(k_t[...], ds, 1, 0) * scale).astype(BF16)
+            dk = dot(ds, q_main[i], 1, 0)
+            dv = dot(p, do, 1, 0)
             if i == 0:
                 dk_acc[...] = dk
                 dv_acc[...] = dv
@@ -454,7 +465,8 @@
     relayed(d_cols, y_mate, s_cb, r_cb)
     relay(d_cols.at[y_mate], d_cols, y_mate, core_mate, s_cb.at[2], r_cb)
 
-    own = jnp.concatenate([att_all[b, h] for h in range(HEAD_GRP)], axis=1)
+    own = jnp.concatenate([att_all[b, h] for h in range(HEAD_GRP)], axis=0)
+    own = jnp.transpose(own.astype(F32)).astype(BF16)
     for p in range(n_grp):
         rs_send[p] = dot(own, w_ref[:, p * feat : (p + 1) * feat], 1, 0).astype(BF16)
     for n, p in enumerate((diagonal, core_mate)):
@@ -504,16 +516,12 @@
     relayed(d_cols, diagonal, s_cb, r_cb)
     for j in range(nz):
         landed(always, 2 * j + 1 - x)
-    grads = d_cols[...].reshape(seq, cols)
+    grads = jnp.concatenate(
+        [d_cols[p, t] for t in range(blocks) for p in range(n_grp)], axis=0
+    )
     for h in range(HEAD_GRP):
-        att = jnp.concatenate(
-            [
-                att_all[:, h, p * quarter : (p + 1) * quarter, :].reshape(blocks * quarter, HD)
-                for p in range(n_grp)
-            ],
-            axis=0,
-        )
-        dw_ref[h] = dot(att, grads, 0, 0)
+        att = jnp.concatenate([att_all[t, h] for t in range(blocks)], axis=1)
+        dw_ref[h] = dot(att, grads, 1, 0)
         write(dw_ref.at[h], dw_out.at[h * HD : (h + 1) * HD])
 
     for n, out in enumerate((dq_out, dk_out, dv_out)):
@@ -581,9 +589,11 @@
             pltpu.VMEM((blocks, rows, HD), BF16),
             pltpu.VMEM((4, step, HD), BF16),
             pltpu.VMEM((n_grp, blocks, rows // n_grp, cols), BF16),
+            pltpu.VMEM((4, seq, step), BF16),
             pltpu.VMEM((4, step, seq), BF16),
             pltpu.VMEM((4, step, seq), BF16),
-            pltpu.VMEM((4, step, seq), BF16),
+            pltpu.VMEM((HD, seq), BF16),
+            pltpu.VMEM((HD, seq), BF16),
             pltpu.VMEM((4, step, HD), BF16),
             pltpu.VMEM((blocks, rows, HD), BF16),
             pltpu.VMEM((blocks, HEAD_GRP, rows, HD), BF16),

time: 52.8 us -> 52.8 us (level)
  no operation moved by 1% of the time
where the time goes in v5:
time: 52.8 us; the launch traced here: 52.6 us
  Pallas kernels  52 us (98%)
  between operations  0.64 us (1%)
    pallas_call x1, Pallas kernels, on_device_fused(): pl.pallas_call(fused_kernel, out_shape=(jax.ShapeDtypeStruct((rows, feat)...  49.7 us
    pallas_call x1, Pallas kernels, on_device_fused(): pl.pallas_call(write_kernel, out_shape=tuple((jax.ShapeDtypeStruct(r.shap...  2.22 us

profile of v5, /device:TPU:0, one launch (start us, length us, event | category | flops | bytes accessed | tf_op | source)
XLA Modules:
  0.0 52.6 jit_solution(3833403997211741132)
XLA Ops:
  0.6 49.7 %shard_map.110 = (bf16[128,768]{1,0:T(8,128)(2,1)}, bf16[128,384]{1,0:T(8,128)(2,1)}, bf16[128,384]{1,0:T(8,128)(2,1)}, bf16[128,384]{1,0:T(8,128)(2,1)}, f32[384,384]{1,0:T(8,128)}) custom-call(bf16[128,768]{1,0:T(8,128)(2,1)} %hidden_hbm.1, bf16[128,384]{1,0:T(8,128)(2,1)} %q_ref.1, bf16[128,384]{1,0:T(8,128)(2,1)} %k_ref.1, bf16[128,384]{1,0:T(8,128)(2,1)} %v_ref.1, ...), custom_call_target="tpu_custom_call" | custom-call | flops 1342177280 | bytes 16777216 | tf_op jit(solution)/shard_map/pallas_call | solution.py:572
  50.4 2.2 %shard_map.111 = (bf16[128,768]{1,0:T(8,128)(2,1)}, bf16[128,384]{1,0:T(8,128)(2,1)}, bf16[128,384]{1,0:T(8,128)(2,1)}, bf16[128,384]{1,0:T(8,128)(2,1)}, f32[384,384]{1,0:T(8,128)}) custom-call(bf16[128,768]{1,0:T(8,128)(2,1)} %get-tuple-element.10.refs_0_, bf16[128,384]{1,0:T(8,128)(2,1)} %get-tuple-element.11.refs_1_, ...), custom_call_target="tpu_custom_call" | custom-call | tf_op jit(solution)/shard_map/pallas_call | solution.py:618

commit v6 on v5

--- a/solution.py
+++ b/solution.py
@@ -163,7 +163,7 @@
     mixed_out, dq_out, dk_out, dv_out, dw_out, mixed_ref, dw_ref, hidden_ref, w_ref,
     dm_full, qkv_in, slots_in, dp_send, do_in, q_main, d_cols,
     probs, place, place_t, k_t, v_t, dq_main, att_send, att_all, rs_send, rs_pass, rs_in,
-    dk_acc, dv_acc, grad_send, grad_in,
+    dq_acc, delta_row, grad_send, grad_in,
     s_dm, s_qkv, s_slot, s_do, s_ca, s_cb, s_at, s_ag, s_rs, s_gr, s_in, s_out,
     r_dm, r_qkv, r_slot, r_do, r_ca, r_cb, r_at, r_ag, r_rs, r_gr,
 ):
@@ -378,51 +378,50 @@
     relay(d_cols.at[g], d_cols, g, y_mate, s_cb.at[0], r_cb)
     relay(d_cols.at[g], d_cols, g, core_mate, s_cb.at[1], r_cb)
 
-    def backward(i):
-        @pl.when(is_owner)
-        def _():
-            for t in range(i * per, (i + 1) * per):
-
-                @pl.when(b != t)
-                def _(t=t):
-                    remote(do_in.at[t], do_in.at[t], s_do.at[0], r_do.at[t], {"blk": t}).wait_recv()
-
-            do = do_in[i * per : (i + 1) * per].reshape(step, HD)
-            delta = jnp.concatenate(
-                [
-                    jnp.sum(
-                        jnp.transpose(do_in[t].astype(F32)) * att_send[t].astype(F32),
-                        axis=0, keepdims=True,
-                    )
-                    for t in range(i * per, (i + 1) * per)
-                ],
-                axis=1,
-            )
-            p = probs[i]
-            d_probs = dot(qkv_in[2].reshape(seq, HD), do, 1, 1)
-            ds = (p.astype(F32) * (d_probs - delta)).astype(BF16)
-            dq_main[i] = jnp.transpose(dot(k_t[...], ds, 1, 0) * scale).astype(BF16)
-            dk = dot(ds, q_main[i], 1, 0)
-            dv = dot(p, do, 1, 0)
-            if i == 0:
-                dk_acc[...] = dk
-                dv_acc[...] = dv
-            elif i < chunks - 1:
-                dk_acc[...] += dk
-                dv_acc[...] += dv
-            else:
-                dk = ((dk_acc[...] + dk) * scale).astype(BF16)
-                grad_send[1] = dk.reshape(blocks, rows, HD)
-                grad_send[2] = (dv_acc[...] + dv).astype(BF16).reshape(blocks, rows, HD)
-
-    def send_grads(n):
-        for t in range(blocks):
+    def send_grads(n, first, count):
+        for t in range(first, first + count):
             send(
                 is_owner & (b != t),
                 lambda t=t: remote(
                     grad_send.at[n, t], grad_in.at[n, mine], s_gr.at[n, t], r_gr.at[n, mine], {"blk": t}
                 ),
             )
+
+    def backward(j):
+        @pl.when(is_owner)
+        def _():
+            if j == 0:
+                for t in range(blocks):
+
+                    @pl.when(b != t)
+                    def _(t=t):
+                        remote(
+                            do_in.at[t], do_in.at[t], s_do.at[0], r_do.at[t], {"blk": t}
+                        ).wait_recv()
+
+                for t in range(blocks):
+                    both = jnp.transpose(do_in[t].astype(F32)) * att_send[t].astype(F32)
+                    delta_row[:, t * rows : (t + 1) * rows] = jnp.sum(both, axis=0, keepdims=True)
+            do = do_in[...].reshape(seq, HD)
+            p = jnp.concatenate(
+                [probs[i, j * step : (j + 1) * step] for i in range(chunks)], axis=1
+            )
+            d_probs = dot(qkv_in[2, j * per : (j + 1) * per].reshape(step, HD), do, 1, 1)
+            ds = (p.astype(F32) * (d_probs - delta_row[...])).astype(BF16)
+            dk = (dot(ds, q_main[...].reshape(seq, HD), 1, 0) * scale).astype(BF16)
+            dv = dot(p, do, 1, 0).astype(BF16)
+            grad_send[1, j * per : (j + 1) * per] = dk.reshape(per, rows, HD)
+            grad_send[2, j * per : (j + 1) * per] = dv.reshape(per, rows, HD)
+            dq_t = dot(k_t[:, j * step : (j + 1) * step], ds, 1, 0)
+            if j == 0:
+                dq_acc[...] = dq_t
+            elif j < chunks - 1:
+                dq_acc[...] += dq_t
+            else:
+                dq_main[...] = jnp.transpose((dq_acc[...] + dq_t) * scale).astype(BF16)
+
+        send_grads(1, j * per, per)
+        send_grads(2, j * per, per)
 
     backward(0)
     for h in range(HEAD_GRP):
@@ -489,15 +488,13 @@
         lambda: remote(rs_pass, rs_in.at[2], s_rs.at[2], r_rs.at[2], {"grp": y_mate}),
     )
     backward(3)
-    send_grads(1)
-    send_grads(2)
 
     @pl.when(is_owner)
     def _():
-        turned = dot(place[...].reshape(seq, seq), dq_main[...].reshape(seq, HD), 1, 0)
+        turned = dot(place[...].reshape(seq, seq), dq_main[...], 1, 0)
         grad_send[0] = turned.astype(BF16).reshape(blocks, rows, HD)
 
-    send_grads(0)
+    send_grads(0, 0, blocks)
     gather_step(3)
 
     @pl.when(is_owner)
@@ -594,14 +591,14 @@
             pltpu.VMEM((4, step, seq), BF16),
             pltpu.VMEM((HD, seq), BF16),
             pltpu.VMEM((HD, seq), BF16),
-            pltpu.VMEM((4, step, HD), BF16),
+            pltpu.VMEM((seq, HD), BF16),
             pltpu.VMEM((blocks, rows, HD), BF16),
             pltpu.VMEM((blocks, HEAD_GRP, rows, HD), BF16),
             pltpu.VMEM((n_grp, rows, feat), BF16),
             pltpu.VMEM((rows, feat), BF16),
             pltpu.VMEM((3, rows, feat), BF16),
-            pltpu.VMEM((seq, HD), F32),
-            pltpu.VMEM((seq, HD), F32),
+            pltpu.VMEM((HD, seq), F32),
+            pltpu.VMEM((1, seq), F32),
             pltpu.VMEM((3, blocks, rows, HD), BF16),
             pltpu.VMEM((3, HEAD_GRP, rows, HD), BF16),
         ] + sems,

time: 52.8 us -> 53.8 us (1.019)
  Pallas kernels: 52 us -> 53 us
    pallas_call x1, Pallas kernels: 49.7 us -> 50.8 us  [on_device_fused(): pl.pallas_call(fused_kernel, out_shape=(jax.ShapeDtypeStruct((rows, feat)...]
where the time goes in v6:
time: 53.8 us; the launch traced here: 53.6 us
  Pallas kernels  53 us (99%)
  between operations  0.64 us (1%)
    pallas_call x1, Pallas kernels, on_device_fused(): pl.pallas_call(fused_kernel, out_shape=(jax.ShapeDtypeStruct((rows, feat)...  50.8 us
    pallas_call x1, Pallas kernels, on_device_fused(): pl.pallas_call(write_kernel, out_shape=tuple((jax.ShapeDtypeStruct(r.shap...  2.22 us

profile of v6, /device:TPU:0, one launch (start us, length us, event | category | flops | bytes accessed | tf_op | source)
XLA Modules:
  0.0 53.6 jit_solution(8950436708628308608)
XLA Ops:
  0.6 50.8 %shard_map.110 = (bf16[128,768]{1,0:T(8,128)(2,1)}, bf16[128,384]{1,0:T(8,128)(2,1)}, bf16[128,384]{1,0:T(8,128)(2,1)}, bf16[128,384]{1,0:T(8,128)(2,1)}, f32[384,384]{1,0:T(8,128)}) custom-call(bf16[128,768]{1,0:T(8,128)(2,1)} %hidden_hbm.1, bf16[128,384]{1,0:T(8,128)(2,1)} %q_ref.1, bf16[128,384]{1,0:T(8,128)(2,1)} %k_ref.1, bf16[128,384]{1,0:T(8,128)(2,1)} %v_ref.1, ...), custom_call_target="tpu_custom_call" | custom-call | flops 1342177280 | bytes 16777216 | tf_op jit(solution)/shard_map/pallas_call | solution.py:569
  51.4 2.2 %shard_map.111 = (bf16[128,768]{1,0:T(8,128)(2,1)}, bf16[128,384]{1,0:T(8,128)(2,1)}, bf16[128,384]{1,0:T(8,128)(2,1)}, bf16[128,384]{1,0:T(8,128)(2,1)}, f32[384,384]{1,0:T(8,128)}) custom-call(bf16[128,768]{1,0:T(8,128)(2,1)} %get-tuple-element.10.refs_0_, bf16[128,384]{1,0:T(8,128)(2,1)} %get-tuple-element.11.refs_1_, ...), custom_call_target="tpu_custom_call" | custom-call | tf_op jit(solution)/shard_map/pallas_call | solution.py:615

commit v7 on v5

--- a/solution.py
+++ b/solution.py
@@ -183,7 +183,7 @@
     nz = blocks // 2
     mate = b + 1 - 2 * x
     core_mate, y_mate, diagonal = g + 1 - 2 * c, (g + 2) % n_grp, n_grp - 1 - g
-    owners = [2 + 2 * c, 5 - 2 * c, 7 * c]
+    owners = [2 + 2 * c, 5 - 5 * c, 3 + 4 * c]
     mine = jnp.where(b == owners[1], 1, jnp.where(b == owners[2], 2, 0))
     is_owner = (b == owners[0]) | (b == owners[1]) | (b == owners[2])
     always = b >= 0
@@ -460,8 +460,8 @@
         pass_on(high & (z > 0), b + 2 * s, b - 2, 4 * s + 2)
         pass_on(high, b + 2 * s, mate, 4 * s + 3)
 
+    gather_step(1)
     backward(1)
-    gather_step(1)
     relayed(d_cols, y_mate, s_cb, r_cb)
     relay(d_cols.at[y_mate], d_cols, y_mate, core_mate, s_cb.at[2], r_cb)
 
@@ -480,14 +480,15 @@
     def rs_landed(n):
         arrive(always, lambda: remote(rs_in.at[n], rs_in.at[n], s_rs.at[0], r_rs.at[n], {"grp": y_mate}))
 
+    gather_step(2)
     backward(2)
-    gather_step(2)
     rs_landed(0)
     rs_pass[...] = (rs_send[y_mate].astype(F32) + rs_in[0].astype(F32)).astype(BF16)
     send(
         always,
         lambda: remote(rs_pass, rs_in.at[2], s_rs.at[2], r_rs.at[2], {"grp": y_mate}),
     )
+    gather_step(3)
     backward(3)
     send_grads(1)
     send_grads(2)
@@ -498,7 +499,6 @@
         grad_send[0] = turned.astype(BF16).reshape(blocks, rows, HD)
 
     send_grads(0)
-    gather_step(3)
 
     @pl.when(is_owner)
     def _():

time: 52.8 us -> 52 us (0.985)
  Pallas kernels: 52 us -> 51.2 us
    pallas_call x1, Pallas kernels: 49.7 us -> 48.9 us  [on_device_fused(): pl.pallas_call(fused_kernel, out_shape=(jax.ShapeDtypeStruct((rows, feat)...]
where the time goes in v7:
time: 52 us; the launch traced here: 51.8 us
  Pallas kernels  51.2 us (98%)
  between operations  0.64 us (1%)
    pallas_call x1, Pallas kernels, on_device_fused(): pl.pallas_call(fused_kernel, out_shape=(jax.ShapeDtypeStruct((rows, feat)...  48.9 us
    pallas_call x1, Pallas kernels, on_device_fused(): pl.pallas_call(write_kernel, out_shape=tuple((jax.ShapeDtypeStruct(r.shap...  2.22 us

profile of v7, /device:TPU:0, one launch (start us, length us, event | category | flops | bytes accessed | tf_op | source)
XLA Modules:
  0.0 51.8 jit_solution(2806144348387981265)
XLA Ops:
  0.6 48.9 %shard_map.110 = (bf16[128,768]{1,0:T(8,128)(2,1)}, bf16[128,384]{1,0:T(8,128)(2,1)}, bf16[128,384]{1,0:T(8,128)(2,1)}, bf16[128,384]{1,0:T(8,128)(2,1)}, f32[384,384]{1,0:T(8,128)}) custom-call(bf16[128,768]{1,0:T(8,128)(2,1)} %hidden_hbm.1, bf16[128,384]{1,0:T(8,128)(2,1)} %q_ref.1, bf16[128,384]{1,0:T(8,128)(2,1)} %k_ref.1, bf16[128,384]{1,0:T(8,128)(2,1)} %v_ref.1, ...), custom_call_target="tpu_custom_call" | custom-call | flops 1342177280 | bytes 16777216 | tf_op jit(solution)/shard_map/pallas_call | solution.py:572
  49.6 2.2 %shard_map.111 = (bf16[128,768]{1,0:T(8,128)(2,1)}, bf16[128,384]{1,0:T(8,128)(2,1)}, bf16[128,384]{1,0:T(8,128)(2,1)}, bf16[128,384]{1,0:T(8,128)(2,1)}, f32[384,384]{1,0:T(8,128)}) custom-call(bf16[128,768]{1,0:T(8,128)(2,1)} %get-tuple-element.10.refs_0_, bf16[128,384]{1,0:T(8,128)(2,1)} %get-tuple-element.11.refs_1_, ...), custom_call_target="tpu_custom_call" | custom-call | tf_op jit(solution)/shard_map/pallas_call | solution.py:618

commit v8 on v6

--- a/solution.py
+++ b/solution.py
@@ -183,7 +183,7 @@
     nz = blocks // 2
     mate = b + 1 - 2 * x
     core_mate, y_mate, diagonal = g + 1 - 2 * c, (g + 2) % n_grp, n_grp - 1 - g
-    owners = [2 + 2 * c, 5 - 2 * c, 7 * c]
+    owners = [2 + 2 * c, 5 - 5 * c, 3 + 4 * c]
     mine = jnp.where(b == owners[1], 1, jnp.where(b == owners[2], 2, 0))
     is_owner = (b == owners[0]) | (b == owners[1]) | (b == owners[2])
     always = b >= 0
@@ -420,6 +420,7 @@
             else:
                 dq_main[...] = jnp.transpose((dq_acc[...] + dq_t) * scale).astype(BF16)
 
+    def send_block(j):
         send_grads(1, j * per, per)
         send_grads(2, j * per, per)
 
@@ -459,8 +460,8 @@
         pass_on(high & (z > 0), b + 2 * s, b - 2, 4 * s + 2)
         pass_on(high, b + 2 * s, mate, 4 * s + 3)
 
+    gather_step(1)
     backward(1)
-    gather_step(1)
     relayed(d_cols, y_mate, s_cb, r_cb)
     relay(d_cols.at[y_mate], d_cols, y_mate, core_mate, s_cb.at[2], r_cb)
 
@@ -479,15 +480,20 @@
     def rs_landed(n):
         arrive(always, lambda: remote(rs_in.at[n], rs_in.at[n], s_rs.at[0], r_rs.at[n], {"grp": y_mate}))
 
+    gather_step(2)
+    send_block(0)
+    send_block(1)
     backward(2)
-    gather_step(2)
     rs_landed(0)
     rs_pass[...] = (rs_send[y_mate].astype(F32) + rs_in[0].astype(F32)).astype(BF16)
     send(
         always,
         lambda: remote(rs_pass, rs_in.at[2], s_rs.at[2], r_rs.at[2], {"grp": y_mate}),
     )
+    gather_step(3)
+    send_block(2)
     backward(3)
+    send_block(3)
 
     @pl.when(is_owner)
     def _():
@@ -495,7 +501,6 @@
         grad_send[0] = turned.astype(BF16).reshape(blocks, rows, HD)
 
     send_grads(0, 0, blocks)
-    gather_step(3)
 
     @pl.when(is_owner)
     def _():

time: 53.8 us -> 53.1 us (0.987)
  Pallas kernels: 53 us -> 52.3 us
    pallas_call x1, Pallas kernels: 50.8 us -> 50.1 us  [on_device_fused(): pl.pallas_call(fused_kernel, out_shape=(jax.ShapeDtypeStruct((rows, feat)...]
where the time goes in v8:
time: 53.1 us; the launch traced here: 52.9 us
  Pallas kernels  52.3 us (98%)
  between operations  0.64 us (1%)
    pallas_call x1, Pallas kernels, on_device_fused(): pl.pallas_call(fused_kernel, out_shape=(jax.ShapeDtypeStruct((rows, feat)...  50.1 us
    pallas_call x1, Pallas kernels, on_device_fused(): pl.pallas_call(write_kernel, out_shape=tuple((jax.ShapeDtypeStruct(r.shap...  2.22 us

profile of v8, /device:TPU:0, one launch (start us, length us, event | category | flops | bytes accessed | tf_op | source)
XLA Modules:
  0.0 52.9 jit_solution(1855280257201921870)
XLA Ops:
  0.6 50.1 %shard_map.110 = (bf16[128,768]{1,0:T(8,128)(2,1)}, bf16[128,384]{1,0:T(8,128)(2,1)}, bf16[128,384]{1,0:T(8,128)(2,1)}, bf16[128,384]{1,0:T(8,128)(2,1)}, f32[384,384]{1,0:T(8,128)}) custom-call(bf16[128,768]{1,0:T(8,128)(2,1)} %hidden_hbm.1, bf16[128,384]{1,0:T(8,128)(2,1)} %q_ref.1, bf16[128,384]{1,0:T(8,128)(2,1)} %k_ref.1, bf16[128,384]{1,0:T(8,128)(2,1)} %v_ref.1, ...), custom_call_target="tpu_custom_call" | custom-call | flops 1342177280 | bytes 16777216 | tf_op jit(solution)/shard_map/pallas_call | solution.py:574
  50.7 2.2 %shard_map.111 = (bf16[128,768]{1,0:T(8,128)(2,1)}, bf16[128,384]{1,0:T(8,128)(2,1)}, bf16[128,384]{1,0:T(8,128)(2,1)}, bf16[128,384]{1,0:T(8,128)(2,1)}, f32[384,384]{1,0:T(8,128)}) custom-call(bf16[128,768]{1,0:T(8,128)(2,1)} %get-tuple-element.10.refs_0_, bf16[128,384]{1,0:T(8,128)(2,1)} %get-tuple-element.11.refs_1_, ...), custom_call_target="tpu_custom_call" | custom-call | tf_op jit(solution)/shard_map/pallas_call | solution.py:620
